TPU v7x, 32 devices: a whole 2x2x4 slice. The times are simulated.
32 devices in a mesh: seq: 4 (over x, core), dp: 8 (over z, y).
Axes of the slice: x: 2, y: 2, z: 4, core: 2. Of those that a mesh axis runs over, the one named last changes fastest.
Arguments:
- queries: bfloat16 [8, 512, 4096], P('dp', 'seq'), may hold values from -4.5 to 4.5
- rotated_key_matrix: bfloat16 [8, 512, 1024], P('dp', 'seq'), may hold values from -4.5 to 4.5
- value_matrix: bfloat16 [8, 512, 1024], P('dp', 'seq'), may hold values from -6 to 6
- out_weight: bfloat16 [4096, 2048], P('seq'), may hold values from -0.09375 to 0.09375
- out_grad: bfloat16 [8, 512, 2048], P('dp', 'seq'), may hold values from -6 to 6
- lengths: int32 [8, 16], P('dp'), may hold values from 1 to 128, 512 in all within a row
- pack_order: int32 [8, 16], P('dp'), may hold values from 0 to 15, each once within a row
Outputs:
- layer_out: bfloat16 [8, 512, 2048], P('dp', 'seq')
- query_grad: bfloat16 [8, 512, 4096], P('dp', 'seq')
- key_grad: bfloat16 [8, 512, 1024], P('dp', 'seq')
- value_grad: bfloat16 [8, 512, 1024], P('dp', 'seq')
- weight_grad: float32 [4096, 2048], P('seq', 'dp')
Inputs may be any that keep to these rules, and one draw needn't show every extreme that they name: The 16 lengths of a window sum to 512; the longest is 128. `pack_order`: each row names every sample once.
All inputs are finite; a program needn't handle non-finite values.
Results may differ from a plain program's by a relative error of at most 0.017.
Values may be sent and summed in bfloat16 or wider, within the bound.
A program may use at most 128 MiB of HBM per device.

v0:
```python
import jax
import jax.numpy as jnp
from jax import lax
from jax.sharding import PartitionSpec as P

QUERY_HEADS = 32
KEY_VALUE_HEADS = 8
HEAD_SIZE = 128


def row_starts(lengths, pack_order, win_rows):
    samples = lengths.shape[0]
    picked = jnp.sum(
        jnp.where(
            pack_order[:, None] == jnp.arange(samples, dtype=jnp.int32)[None, :],
            lengths[None, :],
            0,
        ),
        axis=1,
        dtype=jnp.int32,
    )
    seg_ends = jnp.cumsum(picked, dtype=jnp.int32)
    places = jnp.arange(win_rows, dtype=jnp.int32)
    return jnp.sum(
        jnp.where(seg_ends[None, :] <= places[:, None], picked[None, :], 0), axis=1, dtype=jnp.int32
    )


def local(queries, rotated_key_matrix, value_matrix, out_weight, out_grad, lengths, pack_order):
    row_total_count = queries.shape[1]
    head_scale = HEAD_SIZE ** (-0.5)
    q_tok = queries.reshape(row_total_count, QUERY_HEADS, HEAD_SIZE)
    key_token_rows = rotated_key_matrix.reshape(row_total_count, KEY_VALUE_HEADS, HEAD_SIZE)
    value_token_rows = value_matrix.reshape(row_total_count, KEY_VALUE_HEADS, HEAD_SIZE)
    q_loc, k_loc, v_loc = (
        lax.all_to_all(q_tok, "seq", split_axis=1, concat_axis=0, tiled=True),
        lax.all_to_all(key_token_rows, "seq", split_axis=1, concat_axis=0, tiled=True),
        lax.all_to_all(value_token_rows, "seq", split_axis=1, concat_axis=0, tiled=True),
    )
    win_rows = q_loc.shape[0]
    kv_local = k_loc.shape[1]
    group_width = q_loc.shape[1] // kv_local
    query_head_rows = q_loc.reshape(win_rows, kv_local, group_width, HEAD_SIZE)
    starts = row_starts(lengths[0], pack_order[0], win_rows)
    block_rows = min(512, win_rows)
    blk_count = win_rows // block_rows

    def blk_bounds():
        return (jnp.int32(0), jnp.int32(blk_count))

    def score_tile(q_blk, q_start, k_start):
        k_tile = lax.dynamic_slice_in_dim(k_loc, k_start, block_rows, 0)
        scores = (
            jnp.einsum("qkgd,skd->kgqs", q_blk, k_tile, preferred_element_type=jnp.float32)
            * head_scale
        )
        rows_at = q_start + jnp.arange(block_rows, dtype=jnp.int32)
        cols_at = k_start + jnp.arange(block_rows, dtype=jnp.int32)
        first_at = lax.dynamic_slice_in_dim(starts, q_start, block_rows, 0)
        visible = (cols_at[None, :] >= first_at[:, None]) & (cols_at[None, :] <= rows_at[:, None])
        return (scores, visible)

    def forward_block(blk_index):
        q_start = blk_index * block_rows
        q_blk = lax.dynamic_slice_in_dim(query_head_rows, q_start, block_rows, 0)
        lower_blk, upper_blk = blk_bounds()

        def gather_stats(k_blk, running):
            row_max, row_sum = running
            scores, visible = score_tile(q_blk, q_start, k_blk * block_rows)
            tile_max = jnp.max(jnp.where(visible, scores, -1e30), axis=-1, keepdims=True)
            new_max = jnp.maximum(row_max, tile_max)
            row_sum = row_sum * jnp.exp(row_max - new_max) + jnp.sum(
                jnp.where(visible, jnp.exp(scores - new_max), 0.0), axis=-1, keepdims=True
            )
            return (new_max, row_sum)

        stat_shape = (kv_local, group_width, block_rows, 1)
        row_max, row_sum = lax.fori_loop(
            lower_blk,
            upper_blk,
            gather_stats,
            (jnp.full(stat_shape, -1e30, jnp.float32), jnp.zeros(stat_shape, jnp.float32)),
        )

        def weigh(k_blk, summed):
            k_start = k_blk * block_rows
            scores, visible = score_tile(q_blk, q_start, k_start)
            half_probability = (
                jnp.where(visible, jnp.exp(scores - row_max), 0.0) / row_sum
            ).astype(jnp.bfloat16)
            v_tile = lax.dynamic_slice_in_dim(v_loc, k_start, block_rows, 0)
            return summed + jnp.einsum(
                "kgqs,skd->qkgd", half_probability, v_tile, preferred_element_type=jnp.float32
            )

        summed = lax.fori_loop(
            lower_blk,
            upper_blk,
            weigh,
            jnp.zeros((block_rows, kv_local, group_width, HEAD_SIZE), jnp.float32),
        )
        return (summed.astype(jnp.bfloat16), row_max, row_sum)

    attn_out, max_all, sum_all = lax.map(forward_block, jnp.arange(blk_count, dtype=jnp.int32))
    attn_out = attn_out.reshape(win_rows, kv_local, group_width, HEAD_SIZE)
    a_head = attn_out.reshape(win_rows, kv_local * group_width * HEAD_SIZE)
    grad_rows = out_grad.reshape(row_total_count, out_grad.shape[2])
    a_rows = a_head
    product = jnp.dot(a_rows, out_weight, preferred_element_type=jnp.float32)
    y_out = lax.psum_scatter(
        lax.optimization_barrier(product.astype(jnp.bfloat16))
        .astype(jnp.float32)
        .astype(jnp.bfloat16),
        "seq",
        scatter_dimension=0,
        tiled=True,
    )
    incoming = lax.all_gather(grad_rows, "seq", axis=0, tiled=True)
    a_rows = a_head
    wo_grad = lax.dot_general(
        a_rows, incoming, (((0,), (0,)), ((), ())), preferred_element_type=jnp.float32
    )
    d_rows = lax.dot_general(
        incoming, out_weight, (((1,), (1,)), ((), ())), preferred_element_type=jnp.float32
    )
    d_all, wo_grad = (d_rows, wo_grad)
    attention_grad = d_all.astype(jnp.bfloat16).reshape(win_rows, kv_local, group_width, HEAD_SIZE)

    def back_block(blk_index, running):
        dq_all, dk_acc, dv_acc = running
        q_start = blk_index * block_rows
        q_blk = lax.dynamic_slice_in_dim(query_head_rows, q_start, block_rows, 0)
        g_blk = lax.dynamic_slice_in_dim(attention_grad, q_start, block_rows, 0)
        o_blk = lax.dynamic_slice_in_dim(attn_out, q_start, block_rows, 0)
        row_max = max_all[blk_index]
        row_sum = sum_all[blk_index]
        row_dot = jnp.sum(g_blk.astype(jnp.float32) * o_blk.astype(jnp.float32), axis=-1)
        row_dot = jnp.transpose(row_dot, (1, 2, 0))[..., None]
        lower_blk, upper_blk = blk_bounds()

        def per_tile(k_blk, inner):
            dq_acc, dk_run, dv_run = inner
            k_start = k_blk * block_rows
            scores, visible = score_tile(q_blk, q_start, k_start)
            attn_prob = jnp.where(visible, jnp.exp(scores - row_max), 0.0) / row_sum
            k_tile = lax.dynamic_slice_in_dim(k_loc, k_start, block_rows, 0)
            v_tile = lax.dynamic_slice_in_dim(v_loc, k_start, block_rows, 0)
            d_prob = jnp.einsum("qkgd,skd->kgqs", g_blk, v_tile, preferred_element_type=jnp.float32)
            score_gradient = (attn_prob * (d_prob - row_dot) * head_scale).astype(jnp.bfloat16)
            dq_acc = dq_acc + jnp.einsum(
                "kgqs,skd->qkgd", score_gradient, k_tile, preferred_element_type=jnp.float32
            )
            dk_part = jnp.einsum(
                "ubnh,nubr->hur", score_gradient, q_blk, preferred_element_type=jnp.float32
            )
            dv_part = jnp.einsum(
                "ubnh,nubr->hur",
                attn_prob.astype(jnp.bfloat16),
                g_blk,
                preferred_element_type=jnp.float32,
            )
            dk_run = lax.dynamic_update_slice_in_dim(
                dk_run,
                lax.dynamic_slice_in_dim(dk_run, k_start, block_rows, 0) + dk_part,
                k_start,
                0,
            )
            dv_run = lax.dynamic_update_slice_in_dim(
                dv_run,
                lax.dynamic_slice_in_dim(dv_run, k_start, block_rows, 0) + dv_part,
                k_start,
                0,
            )
            return (dq_acc, dk_run, dv_run)

        dq_blk, dk_acc, dv_acc = lax.fori_loop(
            lower_blk,
            upper_blk,
            per_tile,
            (
                jnp.zeros((block_rows, kv_local, group_width, HEAD_SIZE), jnp.float32),
                dk_acc,
                dv_acc,
            ),
        )
        dq_all = lax.dynamic_update_slice_in_dim(dq_all, dq_blk.astype(jnp.bfloat16), q_start, 0)
        return (dq_all, dk_acc, dv_acc)

    dq_all, dk_acc, dv_acc = lax.fori_loop(
        0,
        blk_count,
        back_block,
        (
            jnp.zeros((win_rows, kv_local, group_width, HEAD_SIZE), jnp.bfloat16),
            jnp.zeros((win_rows, kv_local, HEAD_SIZE), jnp.float32),
            jnp.zeros((win_rows, kv_local, HEAD_SIZE), jnp.float32),
        ),
    )
    d_q = dq_all.reshape(win_rows, kv_local * group_width, HEAD_SIZE)
    d_q, key_gradient, value_gradient = (
        lax.all_to_all(d_q, "seq", split_axis=0, concat_axis=1, tiled=True),
        lax.all_to_all(dk_acc.astype(jnp.bfloat16), "seq", split_axis=0, concat_axis=1, tiled=True),
        lax.all_to_all(dv_acc.astype(jnp.bfloat16), "seq", split_axis=0, concat_axis=1, tiled=True),
    )
    weight_grad = lax.psum_scatter(wo_grad, "dp", scatter_dimension=1, tiled=True)
    return (
        y_out.reshape(1, row_total_count, y_out.shape[1]),
        d_q.reshape(1, row_total_count, QUERY_HEADS * HEAD_SIZE),
        key_gradient.reshape(1, row_total_count, KEY_VALUE_HEADS * HEAD_SIZE),
        value_gradient.reshape(1, row_total_count, KEY_VALUE_HEADS * HEAD_SIZE),
        weight_grad,
    )


def solution(mesh):
    in_specs = (
        P("dp", "seq", None),
        P("dp", "seq", None),
        P("dp", "seq", None),
        P("seq", None),
        P("dp", "seq", None),
        P("dp", None),
        P("dp", None),
    )
    out_specs = (
        P("dp", "seq", None),
        P("dp", "seq", None),
        P("dp", "seq", None),
        P("dp", "seq", None),
        P("seq", "dp"),
    )
    return jax.shard_map(local, mesh=mesh, in_specs=in_specs, out_specs=out_specs, check_vma=False)
```

profile of v0, /device:TPU:0, one launch (start us, length us, event | category | flops | bytes accessed | tf_op | source)
XLA Modules:
  0.0 271.8 jit_solution(7915588788345847429)
XLA Ops:
  7.2 0.0 copy-start.4
  7.2 0.0 copy-start.3
  7.2 0.0 all-gather.3.cloned.1.call-start
  7.2 0.7 all-gather.3.cloned.1.call-update
  7.9 1.8 copy.102
  9.7 4.2 %all-to-all-start = ((bf16[128,8,128]{0,2,1:T(8,128)(2,1)}), bf16[128,8,128]{0,2,1:T(8,128)(2,1)S(1)}, u32[]{:S(2)}, u32[]{:S(2)}) async-start(bf16[128,8,128]{0,2,1:T(8,128)(2,1)} %bitcast.3), calls=%async_computation | async-start | bytes 524288 | tf_op jit(solution)/shard_map/all_to_all | solution.py:37
  13.9 1.8 copy.109
  15.7 4.2 %all-to-all-done = bf16[128,8,128]{0,2,1:T(8,128)(2,1)S(1)} async-done(((bf16[128,8,128]{0,2,1:T(8,128)(2,1)}), bf16[128,8,128]{0,2,1:T(8,128)(2,1)S(1)}, u32[]{:S(2)}, u32[]{:S(2)}) %all-to-all-start) | async-done | bytes 262176 | tf_op jit(solution)/shard_map/all_to_all | solution.py:37
  20.0 3.4 %all-to-all-start.2 = ((bf16[128,8,128]{0,2,1:T(8,128)(2,1)}), bf16[128,8,128]{0,2,1:T(8,128)(2,1)S(1)}, u32[]{:S(2)}, u32[]{:S(2)}) async-start(bf16[128,8,128]{0,2,1:T(8,128)(2,1)} %bitcast.16), calls=%async_computation.2 | async-start | bytes 524288 | tf_op jit(solution)/shard_map/all_to_all | solution.py:38
  23.4 1.6 copy.105
  25.0 1.3 copy.106
  26.3 6.2 %all-to-all-done.2 = bf16[128,8,128]{0,2,1:T(8,128)(2,1)S(1)} async-done(((bf16[128,8,128]{0,2,1:T(8,128)(2,1)}), bf16[128,8,128]{0,2,1:T(8,128)(2,1)S(1)}, u32[]{:S(2)}, u32[]{:S(2)}) %all-to-all-start.2) | async-done | bytes 262176 | tf_op jit(solution)/shard_map/all_to_all | solution.py:38
  32.5 3.5 %all-to-all-start.1 = ((bf16[128,32,128]{2,0,1:T(8,128)(2,1)}), bf16[128,32,128]{2,0,1:T(8,128)(2,1)S(1)}, u32[]{:S(2)}, u32[]{:S(2)}) async-start(bf16[128,32,128]{2,0,1:T(8,128)(2,1)} %copy.106), calls=%async_computation.1 | async-start | bytes 2097152 | tf_op jit(solution)/shard_map/all_to_all | solution.py:36
  36.0 0.0 reduce-scatter.3.cloned.1.call-start
  36.1 0.0 copy-done.4
  36.1 0.0 copy-done.3
  36.1 0.2 select_reduce_fusion.1
  36.3 0.1 copy.101
  36.4 0.1 reduce
  36.5 0.1 select_reduce_fusion
  36.6 0.1 fusion.33
  36.8 0.2 copy.104
  37.0 0.2 copy.111
  37.2 0.1 reshape.115
  37.3 13.2 %all-to-all-done.1 = bf16[128,32,128]{2,0,1:T(8,128)(2,1)S(1)} async-done(((bf16[128,32,128]{2,0,1:T(8,128)(2,1)}), bf16[128,32,128]{2,0,1:T(8,128)(2,1)S(1)}, u32[]{:S(2)}, u32[]{:S(2)}) %all-to-all-start.1) | async-done | bytes 1048608 | tf_op jit(solution)/shard_map/all_to_all | solution.py:36
  50.5 0.1 copy.108
  50.6 1.5 fusion.3
  52.1 3.2 %copy-done = f32[2,512,512,4]{2,1,3,0:T(8,128)} copy-done((f32[2,512,512,4]{2,1,3,0:T(8,128)}, f32[2,512,512,4]{2,1,3,0:T(8,128)S(1)}, u32[]{:S(2)}) %copy-start) | copy-done | bytes 8388632
  55.3 1.8 fusion.7
  57.1 0.0 all-gather.3.cloned.1.call-done
  57.1 6.2 %fusion.19 = bf16[512,1024]{1,0:T(8,128)(2,1)} fusion(bf16[1024,2048]{1,0:T(8,128)(2,1)} %param.10, bf16[1,512,2048]{2,1,0:T(8,128)(2,1)} %all-gather.3.cloned.1.call-done), kind=kOutput, calls=%fused_computation.23 | convolution fusion | flops 2148007936 | bytes 7340032 | tf_op jit(solution)/shard_map/dot_general | solution.py:124
  63.3 1.5 copy.113
  64.8 0.0 copy-start.2
  64.8 6.3 %multiply_reduce_fusion = (f32[512,2,4]{0,2,1:T(4,128)S(1)}, bf16[2,4,512,128]{2,3,1,0:T(8,128)(2,1)S(1)}) fusion(bf16[512,1024]{0,1:T(8,128)(2,1)S(1)} %copy.113, f32[2,4,512]{2,1,0:T(4,128)S(1)} %multiply_add_fusion, f32[2,4,512]{2,1,0:T(4,128)S(1)} %broadcast_maximum_fusion, f32[2,512,512,4]{2,1,3,0:T(8,128)} %copy-done, ...), kind=kOutput, calls=%fused_computation.16 | convolution fusion | flops 549974016 | bytes 11059200 | tf_op jit(solution)/shard_map/while/body/eval_jaxpr/while/body/kgqs,skd->qkgd/dot_general | solution.py:93
  71.1 0.0 copy-start.5
  71.1 1.0 copy-done.5
  72.1 3.8 %convolution_convert_fusion = bf16[512,2048]{1,0:T(8,128)(2,1)} fusion(bf16[512,1024]{0,1:T(8,128)(2,1)S(1)} %bitcast.144, bf16[1024,2048]{1,0:T(8,128)(2,1)S(1)} %copy-done.2), kind=kOutput, calls=%fused_computation.11 | convolution fusion | flops 2148532224 | bytes 7340032 | tf_op jit(solution)/shard_map/dot_general | solution.py:110
  75.9 0.0 reduce-scatter.3.cloned.1.call-update
  75.9 0.2 reduce-scatter.5.cloned.1.call-start
  76.1 7.5 %fusion.8 = f32[1024,2048]{1,0:T(8,128)} fusion(bf16[512,1024]{0,1:T(8,128)(2,1)} %bitcast.145, bf16[1,512,2048]{2,1,0:T(8,128)(2,1)} %all-gather.3.cloned.1.call-done), kind=kOutput, calls=%fused_computation.12 | convolution fusion | flops 2147483648 | bytes 11534336 | tf_op jit(solution)/shard_map/dot_general | solution.py:121
  83.6 0.0 reduce-scatter.5.cloned.1.call-update
  83.6 0.2 copy.138
  83.8 6.4 %fusion.30 = bf16[512,2,128]{0,2,1:T(8,128)(2,1)S(1)} fusion(bf16[512,2,4,128]{0,3,2,1:T(8,128)(2,1)S(1)} %bitcast.134, f32[2,512,512,4]{2,1,3,0:T(8,128)} %copy-done, f32[2,4,512]{2,1,0:T(4,128)S(1)} %multiply_add_fusion, f32[2,4,512]{2,1,0:T(4,128)S(1)} %broadcast_maximum_fusion, pred[512,512]{0,1:T(8,128)(4,1)S(1)} %fusion.33), kind=kOutput, calls=%fused_computation.29 | convolution fusion | flops 547487744 | bytes 9994240 | tf_op jit(solution)/shard_map/while/body/eval_jaxpr/while/body/ubnh,nubr->hur/dot_general | solution.py:157
  90.2 0.9 copy.123
  91.1 3.4 %all-to-all-start.5 = ((bf16[512,2,128]{2,1,0:T(2,128)(2,1)}), bf16[512,2,128]{2,1,0:T(2,128)(2,1)S(1)}, u32[]{:S(2)}, u32[]{:S(2)}) async-start(bf16[512,2,128]{2,1,0:T(2,128)(2,1)} %copy.123), calls=%async_computation.6 | async-start | bytes 524288 | tf_op jit(solution)/shard_map/all_to_all | solution.py:204
  94.5 5.3 %fusion.2 = bf16[2,4,512,512]{2,3,1,0:T(8,128)(2,1)S(1)} fusion(f32[2,4,512]{2,1,0:T(4,128)S(1)} %bitcast.146, bf16[512,2,128,1]{2,0,3,1:T(8,128)(2,1)S(1)} %bitcast.139, bf16[512,2,4,128]{0,3,2,1:T(8,128)(2,1)S(1)} %bitcast.135, f32[2,4,512]{2,1,0:T(4,128)S(1)} %multiply_add_fusion, f32[2,4,512]{2,1,0:T(4,128)S(1)} %broadcast_maximum_fusion, ...), kind=kOutput, calls=%fused_computation.3 | convolution fusion | flops 553648128 | bytes 14204928 | tf_op jit(solution)/shard_map/while/body/eval_jaxpr/while/body/qkgd,skd->kgqs/dot_general | solution.py:149
  99.9 0.0 copy-start.1
  99.9 1.9 copy-done.1
  101.8 1.2 fusion.29
  103.1 1.0 copy.120
  104.0 0.0 all-to-all-done.5
  104.0 3.4 %all-to-all-start.4 = ((bf16[512,2,128]{2,1,0:T(2,128)(2,1)}), bf16[512,2,128]{2,1,0:T(2,128)(2,1)S(1)}, u32[]{:S(2)}, u32[]{:S(2)}) async-start(bf16[512,2,128]{2,1,0:T(2,128)(2,1)} %copy.120), calls=%async_computation.5 | async-start | bytes 524288 | tf_op jit(solution)/shard_map/all_to_all | solution.py:203
  107.5 4.0 %convolution_convert_fusion.1 = bf16[2,4,512,128]{3,2,1,0:T(8,128)(2,1)S(1)} fusion(bf16[2,4,512,512]{2,3,1,0:T(8,128)(2,1)} %copy-done.1, bf16[512,2,128,1]{2,0,3,1:T(8,128)(2,1)S(1)} %bitcast.133), kind=kOutput, calls=%fused_computation.21 | convolution fusion | flops 537395200 | bytes 5505024 | tf_op jit(solution)/shard_map/while/body/eval_jaxpr/while/body/kgqs,skd->qkgd/dot_general | solution.py:151
  111.4 1.6 copy.118
  113.1 0.4 all-to-all-done.4
  113.5 3.5 %all-to-all-start.3 = ((bf16[512,8,128]{2,1,0:T(8,128)(2,1)}), bf16[512,8,128]{2,1,0:T(8,128)(2,1)S(1)}, u32[]{:S(2)}, u32[]{:S(2)}) async-start(bf16[512,8,128]{2,1,0:T(8,128)(2,1)} %copy.118), calls=%async_computation.4 | async-start | bytes 2097152 | tf_op jit(solution)/shard_map/all_to_all | solution.py:202
  117.0 0.2 copy.124
  117.2 0.9 reshape.112
  118.1 0.2 copy.121
  118.2 0.9 reshape.111
  119.1 12.3 %all-to-all-done.3 = bf16[512,8,128]{2,1,0:T(8,128)(2,1)S(1)} async-done(((bf16[512,8,128]{2,1,0:T(8,128)(2,1)}), bf16[512,8,128]{2,1,0:T(8,128)(2,1)S(1)}, u32[]{:S(2)}, u32[]{:S(2)}) %all-to-all-start.3) | async-done | bytes 1048608 | tf_op jit(solution)/shard_map/all_to_all | solution.py:202
  131.4 0.2 copy.119
  131.6 1.3 reshape.110
  132.9 132.4 %reduce-scatter.5.cloned.1.call-done = f32[1024,256]{1,0:T(8,128)} async-done(((f32[1024,2048]{1,0:T(8,128)}), f32[1024,256]{1,0:T(8,128)}) %reduce-scatter.5.cloned.1.call-update) | async-done | bytes 1048592 | tf_op jit(solution)/shard_map/reduce_scatter | solution.py:206
  (6 shorter events, 0.1 us)
Async XLA Ops:
  7.2 28.9 %copy-start.4 = (s32[1,16]{1,0:T(1,128)S(1)}, s32[1,16]{1,0:T(1,128)}, u32[]{:S(2)}) copy-start(s32[1,16]{1,0:T(1,128)} %param.13) | copy-start | bytes 196
  7.2 28.9 %copy-start.3 = (s32[1,16]{1,0:T(1,128)S(1)}, s32[1,16]{1,0:T(1,128)}, u32[]{:S(2)}) copy-start(s32[1,16]{1,0:T(1,128)} %param.12) | copy-start | bytes 196
  7.2 49.9 %all-gather.3.cloned.1.call-start = ((), (), s32[]{:S(2)}) async-start(), calls=%async_computation.10 | async-start | bytes 2621440 | tf_op jit(solution)/shard_map/all_gather | solution.py:119
  9.7 10.2 %all-to-all-start = ((bf16[128,8,128]{0,2,1:T(8,128)(2,1)}), bf16[128,8,128]{0,2,1:T(8,128)(2,1)S(1)}, u32[]{:S(2)}, u32[]{:S(2)}) async-start(bf16[128,8,128]{0,2,1:T(8,128)(2,1)} %bitcast.3), calls=%async_computation | async-start | bytes 524288 | tf_op jit(solution)/shard_map/all_to_all | solution.py:37
  20.0 12.5 %all-to-all-start.2 = ((bf16[128,8,128]{0,2,1:T(8,128)(2,1)}), bf16[128,8,128]{0,2,1:T(8,128)(2,1)S(1)}, u32[]{:S(2)}, u32[]{:S(2)}) async-start(bf16[128,8,128]{0,2,1:T(8,128)(2,1)} %bitcast.16), calls=%async_computation.2 | async-start | bytes 524288 | tf_op jit(solution)/shard_map/all_to_all | solution.py:38
  32.5 18.0 %all-to-all-start.1 = ((bf16[128,32,128]{2,0,1:T(8,128)(2,1)}), bf16[128,32,128]{2,0,1:T(8,128)(2,1)S(1)}, u32[]{:S(2)}, u32[]{:S(2)}) async-start(bf16[128,32,128]{2,0,1:T(8,128)(2,1)} %copy.106), calls=%async_computation.1 | async-start | bytes 2097152 | tf_op jit(solution)/shard_map/all_to_all | solution.py:36
  36.0 96.8 %reduce-scatter.3.cloned.1.call-start = ((), (), s32[]{:S(2)}) async-start(), calls=%async_computation.8 | async-start | bytes 2621440 | tf_op jit(solution)/shard_map/reduce_scatter | solution.py:111
  52.1 3.2 %copy-start = (f32[2,512,512,4]{2,1,3,0:T(8,128)}, f32[2,512,512,4]{2,1,3,0:T(8,128)S(1)}, u32[]{:S(2)}) copy-start(f32[2,512,512,4]{2,1,3,0:T(8,128)S(1)} %get-tuple-element.146) | copy-start | bytes 25165828
  64.8 7.3 %copy-start.2 = (bf16[1024,2048]{1,0:T(8,128)(2,1)S(1)}, bf16[1024,2048]{1,0:T(8,128)(2,1)}, u32[]{:S(2)}) copy-start(bf16[1024,2048]{1,0:T(8,128)(2,1)} %param.10) | copy-start | bytes 12582916
  71.1 1.0 copy-start.5
  75.9 189.4 %reduce-scatter.5.cloned.1.call-start = ((), (), s32[]{:S(2)}) async-start(), calls=%async_computation.9 | async-start | bytes 9437184 | tf_op jit(solution)/shard_map/reduce_scatter | solution.py:206
  91.1 13.0 %all-to-all-start.5 = ((bf16[512,2,128]{2,1,0:T(2,128)(2,1)}), bf16[512,2,128]{2,1,0:T(2,128)(2,1)S(1)}, u32[]{:S(2)}, u32[]{:S(2)}) async-start(bf16[512,2,128]{2,1,0:T(2,128)(2,1)} %copy.123), calls=%async_computation.6 | async-start | bytes 524288 | tf_op jit(solution)/shard_map/all_to_all | solution.py:204
  99.9 2.0 copy-start.1
  104.0 9.4 %all-to-all-start.4 = ((bf16[512,2,128]{2,1,0:T(2,128)(2,1)}), bf16[512,2,128]{2,1,0:T(2,128)(2,1)S(1)}, u32[]{:S(2)}, u32[]{:S(2)}) async-start(bf16[512,2,128]{2,1,0:T(2,128)(2,1)} %copy.120), calls=%async_computation.5 | async-start | bytes 524288 | tf_op jit(solution)/shard_map/all_to_all | solution.py:203
  113.5 18.0 %all-to-all-start.3 = ((bf16[512,8,128]{2,1,0:T(8,128)(2,1)}), bf16[512,8,128]{2,1,0:T(8,128)(2,1)S(1)}, u32[]{:S(2)}, u32[]{:S(2)}) async-start(bf16[512,8,128]{2,1,0:T(8,128)(2,1)} %copy.118), calls=%async_computation.4 | async-start | bytes 2097152 | tf_op jit(solution)/shard_map/all_to_all | solution.py:202
Sparse Core Ops, SparseCore 0:
  9.6 28.1 all-gather.2
  76.0 35.1 reduce-scatter.2
  115.9 149.3 reduce-scatter.4
where the time goes:
time: 273 us; the launch traced here: 272 us
  waiting for transfers between devices  169 us (62%)
  matrix products  42.2 us (15%)
  local copies, waits for them, and re-layouts  22 us (8%)
  starting transfers between devices  21.8 us (8%)
  between operations  14 us (5%)
    reduce_scatter x1, waiting for transfers between devices, local(): lax.psum_scatter(wo_grad, 'dp', scatter_dimension=1, tiled=True)  132 us
    all_to_all x1, waiting for transfers between devices, local(): lax.all_to_all(q_tok, 'seq', split_axis=1, concat_axis=0, tiled=True)  13.2 us
    all_to_all x1, waiting for transfers between devices, local(): lax.all_to_all(d_q, 'seq', split_axis=0, concat_axis=1, tiled=True)  12.3 us
    unnamed x15, local copies, waits for them, and re-layouts  11.3 us
    dot_general x1, matrix products, local(): lax.dot_general(a_rows, incoming, (((0,), (0,)), ((), ())), preferred_ele...  7.49 us
    dot_general x1, matrix products, per_tile(): jnp.einsum('ubnh,nubr->hur', attn_prob.astype(jnp.bfloat16), g_blk, prefe...  6.41 us
    dot_general x1, matrix products, weigh(): jnp.einsum('kgqs,skd->qkgd', half_probability, v_tile, preferred_element_...  6.29 us
    all_to_all x1, waiting for transfers between devices, local(): lax.all_to_all(value_token_rows, 'seq', split_axis=1, concat_axis=0, tile...  6.2 us
  transfers between devices with their start and end apart: 9, of which 6 were waited for; matrix products, arithmetic and copies ran while one was open for 16% of the time, Pallas kernels for 0%

commit v1 on v0

v1 whole, which is shorter than its diff:
```python
import functools

import jax
import jax.numpy as jnp
from jax import lax
from jax.experimental import pallas as pl
from jax.experimental.pallas import tpu as pltpu
from jax.sharding import PartitionSpec as P

QUERY_HEADS = 32
KEY_VALUE_HEADS = 8
HEAD_SIZE = 128
GROUP = QUERY_HEADS // KEY_VALUE_HEADS
SCALE = HEAD_SIZE**-0.5


def row_starts(lengths, pack_order, win_rows):
    samples = lengths.shape[0]
    picked = jnp.sum(
        jnp.where(
            pack_order[:, None] == jnp.arange(samples, dtype=jnp.int32)[None, :],
            lengths[None, :],
            0,
        ),
        axis=1,
        dtype=jnp.int32,
    )
    at = jnp.arange(samples, dtype=jnp.int32)
    seg_ends = jnp.sum(jnp.where(at[None, :] <= at[:, None], picked[None, :], 0), axis=1)
    places = jnp.arange(win_rows, dtype=jnp.int32)
    return jnp.sum(
        jnp.where(seg_ends[None, :] <= places[:, None], picked[None, :], 0), axis=1, dtype=jnp.int32
    )


def nt(a, b):
    return lax.dot_general(a, b, (((1,), (1,)), ((), ())), preferred_element_type=jnp.float32)


def tn(a, b):
    return lax.dot_general(a, b, (((0,), (0,)), ((), ())), preferred_element_type=jnp.float32)


def stack_heads(x):
    return jnp.concatenate(
        [x[:, j * HEAD_SIZE : (j + 1) * HEAD_SIZE] for j in range(GROUP)], axis=0
    )


def unstack_heads(x, rows):
    return jnp.concatenate([x[j * rows : (j + 1) * rows] for j in range(GROUP)], axis=1)


def forward_kernel(q_ref, k_ref, v_ref, first_ref, a_ref, p_ref):
    rows, wide = q_ref.shape[0], k_ref.shape[0]
    back = wide - rows
    col = lax.broadcasted_iota(jnp.int32, (rows, wide), 1)
    row = lax.broadcasted_iota(jnp.int32, (rows, wide), 0) + back
    visible = (col >= first_ref[...]) & (col <= row)
    hidden = jnp.where(visible, 0.0, -jnp.inf)
    hidden = jnp.concatenate([hidden] * GROUP, axis=0)
    scores = nt(stack_heads(q_ref[...]), k_ref[...]) * SCALE + hidden
    e = jnp.exp(scores - jnp.max(scores, axis=-1, keepdims=True))
    p = (e / jnp.sum(e, axis=-1, keepdims=True)).astype(jnp.bfloat16)
    p_ref[0] = p
    a = jnp.dot(p, v_ref[...], preferred_element_type=jnp.float32).astype(jnp.bfloat16)
    a_ref[...] = unstack_heads(a, rows)


def backward_kernel(q_ref, k_ref, v_ref, a_ref, g_ref, p_ref, dq_ref, dk_ref, dv_ref):
    rows = q_ref.shape[0]
    q, g = stack_heads(q_ref[...]), stack_heads(g_ref[...])
    a = stack_heads(a_ref[...])
    p = p_ref[0]
    dot = jnp.sum(a.astype(jnp.float32) * g.astype(jnp.float32), axis=-1, keepdims=True)
    dp = nt(g, v_ref[...])
    ds = (p.astype(jnp.float32) * (dp - dot) * SCALE).astype(jnp.bfloat16)
    dq = jnp.dot(ds, k_ref[...], preferred_element_type=jnp.float32).astype(jnp.bfloat16)
    dq_ref[...] = unstack_heads(dq, rows)
    dk_ref[...] = tn(ds, q).astype(dk_ref.dtype)
    dv_ref[...] = tn(p, g).astype(dv_ref.dtype)


def local(n_seq, n_dp, queries, keys, values, out_weight, out_grad, lengths, pack_order):
    q, k, v, g = queries[0], keys[0], values[0], out_grad[0]
    rows = q.shape[0]
    win = rows * n_seq
    longest = win // 4
    halo = -(-(longest - 1) // rows)
    me = lax.axis_index("seq")
    starts = row_starts(lengths[0], pack_order[0], win)
    first = lax.dynamic_slice_in_dim(starts, me * rows, rows, 0) - (me - halo) * rows
    first = first[:, None]

    kv = jnp.concatenate([k, v], axis=1)
    pieces = [kv]
    for j in range(1, halo + 1):
        pieces.insert(0, lax.ppermute(kv, "seq", [(i, i + j) for i in range(n_seq - j)]))
    kv_all = jnp.concatenate(pieces, axis=0)
    wide = kv_all.shape[0]
    g_all = lax.all_gather(g, "seq", axis=0, tiled=True)

    kvw = KEY_VALUE_HEADS * HEAD_SIZE
    gw = GROUP * HEAD_SIZE
    q_spec = pl.BlockSpec((rows, gw), lambda i: (0, i))
    k_spec = pl.BlockSpec((wide, HEAD_SIZE), lambda i: (0, i))
    v_spec = pl.BlockSpec((wide, HEAD_SIZE), lambda i: (0, i + KEY_VALUE_HEADS))
    p_spec = pl.BlockSpec((1, GROUP * rows, wide), lambda i: (i, 0, 0))
    params = pltpu.CompilerParams(vmem_limit_bytes=32 << 20)
    a, p = pl.pallas_call(
        forward_kernel,
        grid=(KEY_VALUE_HEADS,),
        in_specs=[q_spec, k_spec, v_spec, pl.BlockSpec((rows, 1), lambda i: (0, 0))],
        out_specs=[q_spec, p_spec],
        out_shape=[
            jax.ShapeDtypeStruct(q.shape, jnp.bfloat16),
            jax.ShapeDtypeStruct((KEY_VALUE_HEADS, GROUP * rows, wide), jnp.bfloat16),
        ],
        compiler_params=params,
        name="attention_forward",
    )(q, kv_all, kv_all, first)

    d_all = lax.dot_general(
        g_all, out_weight, (((1,), (1,)), ((), ())), preferred_element_type=jnp.float32
    ).astype(jnp.bfloat16)
    a_all = lax.all_to_all(a, "seq", split_axis=1, concat_axis=0, tiled=True)
    d = lax.all_to_all(d_all, "seq", split_axis=0, concat_axis=1, tiled=True)

    wo_grad = lax.dot_general(
        a_all, g_all, (((0,), (0,)), ((), ())), preferred_element_type=jnp.float32
    ).astype(jnp.bfloat16)
    weight_grad = lax.psum_scatter(wo_grad, "dp", scatter_dimension=1, tiled=True)
    product = jnp.dot(a_all, out_weight, preferred_element_type=jnp.float32)
    y = lax.psum_scatter(product.astype(jnp.bfloat16), "seq", scatter_dimension=0, tiled=True)

    k_out = pl.BlockSpec((wide, HEAD_SIZE), lambda i: (0, i))
    dq, dk, dv = pl.pallas_call(
        backward_kernel,
        grid=(KEY_VALUE_HEADS,),
        in_specs=[q_spec, k_spec, v_spec, q_spec, q_spec, p_spec],
        out_specs=[q_spec, k_out, k_out],
        out_shape=[
            jax.ShapeDtypeStruct(q.shape, jnp.bfloat16),
            jax.ShapeDtypeStruct((wide, kvw), jnp.bfloat16),
            jax.ShapeDtypeStruct((wide, kvw), jnp.bfloat16),
        ],
        compiler_params=params,
        name="attention_backward",
    )(q, kv_all, kv_all, a, d, p)
    dkv = jnp.concatenate([dk, dv], axis=1)
    total = dkv[halo * rows :].astype(jnp.float32)
    for j in range(1, halo + 1):
        part = lax.ppermute(
            dkv[(halo - j) * rows : (halo - j + 1) * rows],
            "seq",
            [(i + j, i) for i in range(n_seq - j)],
        )
        total = total + part.astype(jnp.float32)
    total = total.astype(jnp.bfloat16)
    return (
        y[None],
        dq[None],
        total[None, :, :kvw],
        total[None, :, kvw:],
        weight_grad.astype(jnp.float32),
    )


def solution(mesh):
    row = P("dp", "seq", None)
    return jax.shard_map(
        functools.partial(local, mesh.shape["seq"], mesh.shape["dp"]),
        mesh=mesh,
        in_specs=(row, row, row, P("seq", None), row, P("dp", None), P("dp", None)),
        out_specs=(row, row, row, row, P("seq", "dp")),
        check_vma=False,
    )
```

time: 273 us -> 183 us (0.67)
  waiting for transfers between devices: 169 us -> 84.8 us
  blocking collectives: 0 us -> 42.2 us
  matrix products: 42.2 us -> 18 us
  local copies, waits for them, and re-layouts: 22 us -> 2.57 us
  starting transfers between devices: 21.8 us -> 3.8 us
  Pallas kernels: 0 us -> 11.9 us
  other arithmetic: 2.35 us -> 5.53 us
    reduce_scatter x1, waiting for transfers between devices: 132 us -> 49 us  [local(): lax.psum_scatter(wo_grad, 'dp', scatter_dimension=1, tiled=True)]
    all_to_all x0 -> x2, blocking collectives: none -> 42.2 us  [the longest x1 25.2 us: local(): a_all = lax.all_to_all(a, 'seq', split_axis=1, concat_axis=0, tiled=True)]
    all_to_all x6 -> x0, waiting for transfers between devices: 36.3 us -> none  [the longest x1 13.2 us: local(): lax.all_to_all(q_tok, 'seq', split_axis=1, concat_axis=0, tiled=True)]
    reduce_scatter x1, waiting for transfers between devices: 0.01 us -> 32.4 us  [local(): lax.psum_scatter(product.astype(jnp.bfloat16), 'seq', scatter_dimension=0...]
    dot_general x9 -> x3, matrix products: 42.2 us -> 18 us  [the longest x1 6.24 us: local(): lax.dot_general(a_all, g_all, (((0,), (0,)), ((), ())), preferred_element...]
    all_to_all x6 -> x0, starting transfers between devices: 21.5 us -> none  [the longest x1 4.21 us: local(): lax.all_to_all(key_token_rows, 'seq', split_axis=1, concat_axis=0, tiled=...]
    pallas_call x0 -> x2, Pallas kernels: none -> 11.9 us  [the longest x1 6.12 us: local(): pl.pallas_call(backward_kernel, grid=(KEY_VALUE_HEADS,), in_specs=[q_spec...]
    unnamed x15 -> x7, local copies, waits for them, and re-layouts: 11.3 us -> 1.38 us
  transfers between devices with their start and end apart: 9 -> 5, of which waited for: 6 -> 4; matrix products, arithmetic and copies ran while one was open for 16% -> 10% of each run, Pallas kernels for 0% -> 7%
where the time goes in v1:
time: 183 us
  waiting for transfers between devices  84.8 us (46%)
  blocking collectives  42.2 us (23%)
  matrix products  18 us (10%)
  between operations  13.9 us (8%)
  Pallas kernels  11.9 us (7%)
  other arithmetic  5.53 us (3%)
  starting transfers between devices  3.8 us (2%)
  local copies, waits for them, and re-layouts  2.57 us (1%)
    reduce_scatter x1, waiting for transfers between devices, local(): lax.psum_scatter(wo_grad, 'dp', scatter_dimension=1, tiled=True)  49 us
    reduce_scatter x1, waiting for transfers between devices, local(): lax.psum_scatter(product.astype(jnp.bfloat16), 'seq', scatter_dimension=0...  32.4 us
    all_to_all x1, blocking collectives, local(): a_all = lax.all_to_all(a, 'seq', split_axis=1, concat_axis=0, tiled=True)  25.2 us
    all_to_all x1, blocking collectives, local(): d = lax.all_to_all(d_all, 'seq', split_axis=0, concat_axis=1, tiled=True)  17 us
    dot_general x1, matrix products, local(): lax.dot_general(a_all, g_all, (((0,), (0,)), ((), ())), preferred_element...  6.24 us
    dot_general x1, matrix products, local(): product = jnp.dot(a_all, out_weight, preferred_element_type=jnp.float32)  6.22 us
    pallas_call x1, Pallas kernels, local(): pl.pallas_call(backward_kernel, grid=(KEY_VALUE_HEADS,), in_specs=[q_spec...  6.12 us
    pallas_call x1, Pallas kernels, local(): pl.pallas_call(forward_kernel, grid=(KEY_VALUE_HEADS,), in_specs=[q_spec,...  5.76 us
  transfers between devices with their start and end apart: 5, of which 4 were waited for; matrix products, arithmetic and copies ran while one was open for 10% of the time, Pallas kernels for 7%

profile of v1, /device:TPU:0, one launch (start us, length us, event | category | flops | bytes accessed | tf_op | source)
XLA Modules:
  0.0 182.7 jit_solution(12552851717712221625)
XLA Ops:
  7.2 0.0 copy-start
  7.2 0.0 all-gather.3.cloned.1.call-start
  7.2 0.7 all-gather.3.cloned.1.call-update
  7.9 0.0 reduce-scatter.5.cloned.1.call-start
  8.0 1.1 pad_maximum_fusion
  9.0 2.4 %collective-permute-start = (bf16[128,2048]{1,0:T(8,128)(2,1)S(1)}, bf16[128,2048]{1,0:T(8,128)(2,1)S(1)}, u32[]{:S(2)}, u32[]{:S(2)}) collective-permute-start(bf16[128,2048]{1,0:T(8,128)(2,1)S(1)} %pad_maximum_fusion), channel_id=1, source_target_pairs={{0,8},{8,16},{16,24},{1,9},{9,17},{17,25},{2,10},{10,18},{18,26},{... | collective-permute-start | bytes 1572872 | tf_op jit(solution)/shard_map/ppermute | solution.py:98
  11.4 0.9 select_reduce_fusion.2
  12.3 0.1 select_reduce_fusion.1
  12.4 0.1 select_reduce_fusion
  12.5 0.1 subtract_bitcast_fusion
  12.6 0.1 copy.20.first_ref
  12.7 0.2 collective-permute-done
  12.9 1.1 maximum_maximum_fusion.k_ref.v_ref
  14.0 0.0 copy-done
  14.0 5.8 %attention_forward.1 = (bf16[128,4096]{1,0:T(8,128)(2,1)S(1)}, bf16[8,512,256]{2,1,0:T(8,128)(2,1)S(1)}) custom-call(bf16[128,4096]{1,0:T(8,128)(2,1)S(1)} %bitcast.35, bf16[256,2048]{1,0:T(8,128)(2,1)S(1)} %maximum_maximum_fusion.k_ref.v_ref, bf16[256,2048]{1,0:T(8,128)(2,1)S(1)} %maximum_maximum_fusion.k_ref.v_ref, s32[128,1]{1,0:T(8,128)S(1)} %copy.20.first_ref), custom_call_target="tpu_custom_call" | custom-call | tf_op jit(solution)/shard_map/attention_forward/pallas_call | solution.py:110
  19.8 0.0 copy-start.1
  19.8 1.3 copy-done.1
  21.2 0.1 copy.26
  21.2 25.2 %all_to_all.38 = bf16[128,4,1024]{2,0,1:T(8,128)(2,1)} all-to-all(bf16[128,4,1024]{2,0,1:T(8,128)(2,1)S(1)} %bitcast.40), channel_id=1, replica_groups=mesh['seq'=4,'dp'=8] {'seq'}, dimensions={1} | all-to-all | bytes 2097152 | tf_op jit(solution)/shard_map/all_to_all | solution.py:126
  46.4 0.0 all-gather.3.cloned.1.call-done
  46.4 6.2 %convolution_convert_fusion = bf16[1024,2048]{1,0:T(8,128)(2,1)} fusion(bf16[512,1024]{1,0:T(8,128)(2,1)} %bitcast.41, bf16[1,512,2048]{2,1,0:T(8,128)(2,1)} %all-gather.3.cloned.1.call-done), kind=kOutput, calls=%fused_computation | convolution fusion | flops 2149580800 | bytes 7340032 | tf_op jit(solution)/shard_map/dot_general | solution.py:129
  52.7 0.0 reduce-scatter.5.cloned.1.call-update
  52.7 0.0 reduce-scatter.3.cloned.1.call-start
  52.8 6.2 %convolution_convert_fusion.1 = bf16[512,2048]{1,0:T(8,128)(2,1)} fusion(bf16[512,1024]{1,0:T(8,128)(2,1)} %bitcast.42, bf16[1024,2048]{1,0:T(8,128)(2,1)} %param.10), kind=kOutput, calls=%fused_computation.1 | convolution fusion | flops 2148532224 | bytes 7340032 | tf_op jit(solution)/shard_map/dot_general | solution.py:133
  59.0 0.0 reduce-scatter.3.cloned.1.call-update
  59.0 5.6 %fusion.3 = bf16[512,1024]{1,0:T(8,128)(2,1)S(1)} fusion(bf16[1024,2048]{1,0:T(8,128)(2,1)} %param.10, bf16[1,512,2048]{2,1,0:T(8,128)(2,1)} %all-gather.3.cloned.1.call-done), kind=kOutput, calls=%fused_computation.5 | convolution fusion | flops 2148007936 | bytes 7340032 | tf_op jit(solution)/shard_map/dot_general | solution.py:123
  64.6 0.0 copy-start.2
  64.6 17.0 %all_to_all.39 = bf16[4,128,1024]{2,1,0:T(8,128)(2,1)S(1)} all-to-all(bf16[4,128,1024]{2,1,0:T(8,128)(2,1)S(1)} %bitcast.43), channel_id=1, replica_groups=mesh['seq'=4,'dp'=8] {'seq'}, dimensions={0} | all-to-all | bytes 2097152 | tf_op jit(solution)/shard_map/all_to_all | solution.py:127
  81.6 0.1 copy.24
  81.7 0.0 copy-done.2
  81.7 6.1 %attention_backward.1 = (bf16[128,4096]{1,0:T(8,128)(2,1)}, bf16[256,1024]{1,0:T(8,128)(2,1)S(1)}, bf16[256,1024]{1,0:T(8,128)(2,1)S(1)}) custom-call(bf16[128,4096]{1,0:T(8,128)(2,1)S(1)} %bitcast.36, bf16[256,2048]{1,0:T(8,128)(2,1)S(1)} %maximum_maximum_fusion.k_ref.v_ref, bf16[256,2048]{1,0:T(8,128)(2,1)S(1)} %maximum_maximum_fusion.k_ref.v_ref, ...), custom_call_target="tpu_custom_call" | custom-call | tf_op jit(solution)/shard_map/attention_backward/pallas_call | solution.py:137
  88.0 1.3 collective-permute-start.1
  89.3 2.5 %collective-permute-done.1 = bf16[128,2048]{1,0:T(8,128)(2,1)S(1)} collective-permute-done((bf16[128,2048]{1,0:T(8,128)(2,1)S(1)}, bf16[128,2048]{1,0:T(8,128)(2,1)S(1)}, u32[]{:S(2)}, u32[]{:S(2)}) %collective-permute-start.1) | collective-permute-done | bytes 524320 | tf_op jit(solution)/shard_map/ppermute | solution.py:153
  91.8 0.1 add_convert_fusion
  91.9 0.8 slice_bitcast_fusion
  92.7 49.0 %reduce-scatter.5.cloned.1.call-done = bf16[1024,256]{1,0:T(8,128)(2,1)} async-done(((bf16[1024,2048]{1,0:T(8,128)(2,1)}), bf16[1024,256]{1,0:T(8,128)(2,1)}) %reduce-scatter.5.cloned.1.call-update) | async-done | bytes 524304 | tf_op jit(solution)/shard_map/reduce_scatter | solution.py:132
  141.7 2.1 %convert_element_type.27 = f32[1024,256]{1,0:T(8,128)} convert(bf16[1024,256]{1,0:T(8,128)(2,1)} %reduce-scatter.5.cloned.1.call-done) | non-fusion elementwise | flops 262144 | bytes 1572864 | tf_op jit(solution)/shard_map/convert_element_type | solution.py:165
  143.8 32.4 %reduce-scatter.3.cloned.1.call-done = bf16[128,2048]{1,0:T(8,128)(2,1)} async-done(((bf16[512,2048]{1,0:T(8,128)(2,1)}), bf16[128,2048]{1,0:T(8,128)(2,1)}) %reduce-scatter.3.cloned.1.call-update) | async-done | bytes 524304 | tf_op jit(solution)/shard_map/reduce_scatter | solution.py:134
  (3 shorter events, 0.1 us)
Async XLA Ops:
  7.2 6.9 %copy-start = (bf16[1,128,4096]{2,1,0:T(8,128)(2,1)S(1)}, bf16[1,128,4096]{2,1,0:T(8,128)(2,1)}, u32[]{:S(2)}) copy-start(bf16[1,128,4096]{2,1,0:T(8,128)(2,1)} %param.7) | copy-start | bytes 3145732
  7.2 39.3 %all-gather.3.cloned.1.call-start = ((), (), s32[]{:S(2)}) async-start(), calls=%async_computation.6 | async-start | bytes 2621440 | tf_op jit(solution)/shard_map/all_gather | solution.py:101
  7.9 133.8 %reduce-scatter.5.cloned.1.call-start = ((), (), s32[]{:S(2)}) async-start(), calls=%async_computation.5 | async-start | bytes 4718592 | tf_op jit(solution)/shard_map/reduce_scatter | solution.py:132
  9.0 3.9 %collective-permute-start = (bf16[128,2048]{1,0:T(8,128)(2,1)S(1)}, bf16[128,2048]{1,0:T(8,128)(2,1)S(1)}, u32[]{:S(2)}, u32[]{:S(2)}) collective-permute-start(bf16[128,2048]{1,0:T(8,128)(2,1)S(1)} %pad_maximum_fusion), channel_id=1, source_target_pairs={{0,8},{8,16},{16,24},{1,9},{9,17},{17,25},{2,10},{10,18},{18,26},{... | collective-permute-start | bytes 1572872 | tf_op jit(solution)/shard_map/ppermute | solution.py:98
  19.8 1.3 copy-start.1
  52.7 123.4 %reduce-scatter.3.cloned.1.call-start = ((), (), s32[]{:S(2)}) async-start(), calls=%async_computation.4 | async-start | bytes 2621440 | tf_op jit(solution)/shard_map/reduce_scatter | solution.py:134
  64.6 17.1 %copy-start.2 = (bf16[8,512,256]{2,1,0:T(8,128)(2,1)S(1)}, bf16[8,512,256]{2,1,0:T(8,128)(2,1)}, u32[]{:S(2)}) copy-start(bf16[8,512,256]{2,1,0:T(8,128)(2,1)} %copy-done.1) | copy-start | bytes 6291460
  88.0 3.8 %collective-permute-start.1 = (bf16[128,2048]{1,0:T(8,128)(2,1)S(1)}, bf16[128,2048]{1,0:T(8,128)(2,1)S(1)}, u32[]{:S(2)}, u32[]{:S(2)}) collective-permute-start(bf16[128,2048]{1,0:T(8,128)(2,1)S(1)} %slice.17), channel_id=1, source_target_pairs={{8,0},{16,8},{24,16},{9,1},{17,9},{25,17},{10,2},{18,10},{26,18},{... | collective-permute-start | bytes 1572872 | tf_op jit(solution)/shard_map/ppermute | solution.py:153
Sparse Core Ops, SparseCore 0:
  9.6 25.2 all-gather.2
  52.8 88.8 reduce-scatter.4
  145.0 31.1 reduce-scatter.2

commit v2 on v1

--- a/solution.py
+++ b/solution.py
@@ -79,6 +79,63 @@
     dq_ref[...] = unstack_heads(dq, rows)
     dk_ref[...] = tn(ds, q).astype(dk_ref.dtype)
     dv_ref[...] = tn(p, g).astype(dv_ref.dtype)
+
+
+def weight_kernel(order_ref, a_ref, g_ref, o_ref):
+    g = g_ref[0] if len(g_ref.shape) == 3 else g_ref[...]
+    o_ref[0] = tn(a_ref[...], g).astype(o_ref.dtype)
+
+
+def weight_blocks(a_all, g_all, order, part, parts, n_dp):
+    win, cols = g_all.shape
+    wide = cols // n_dp
+    high = a_all.shape[1] // parts
+    if wide % 128:
+        g_all = jnp.transpose(g_all.reshape(win, n_dp, wide), (1, 0, 2))
+        g_spec = pl.BlockSpec((1, win, wide), lambda i, o: (o[i], 0, 0))
+    else:
+        g_spec = pl.BlockSpec((win, wide), lambda i, o: (0, o[i]))
+    count = order.shape[0]
+    return pl.pallas_call(
+        weight_kernel,
+        grid_spec=pltpu.PrefetchScalarGridSpec(
+            num_scalar_prefetch=1,
+            grid=(count,),
+            in_specs=[pl.BlockSpec((win, high), lambda i, o: (0, part)), g_spec],
+            out_specs=pl.BlockSpec((1, high, wide), lambda i, o: (i, 0, 0)),
+        ),
+        out_shape=jax.ShapeDtypeStruct((count, high, wide), jnp.bfloat16),
+        compiler_params=pltpu.CompilerParams(vmem_limit_bytes=32 << 20),
+        cost_estimate=pl.CostEstimate(
+            flops=2 * win * high * wide * count,
+            bytes_accessed=2 * (win * high + win * wide * count + high * wide * count),
+            transcendentals=0,
+        ),
+        name="weight_blocks",
+    )(order, a_all, g_all)
+
+
+def exchange(sent, kept, bit, n_dp):
+    got = lax.ppermute(sent, "dp", [(i, i ^ bit) for i in range(n_dp)])
+    return kept.astype(jnp.float32) + got.astype(jnp.float32)
+
+
+def split_half(total):
+    total = total.astype(jnp.bfloat16)
+    half = total.shape[0] // 2
+    return total[half:], total[:half]
+
+
+def bit_orders(n_dp):
+    bits = [1 << i for i in range(n_dp.bit_length() - 1)]
+    return [bits, [bits[1], bits[0]] + bits[2:]]
+
+
+def offsets(bits):
+    found = [0]
+    for bit in reversed(bits):
+        found = found + [j ^ bit for j in found]
+    return found
 
 
 def local(n_seq, n_dp, queries, keys, values, out_weight, out_grad, lengths, pack_order):
@@ -120,18 +177,35 @@
         name="attention_forward",
     )(q, kv_all, kv_all, first)
 
+    a_all = lax.all_to_all(a, "seq", split_axis=1, concat_axis=0, tiled=True)
     d_all = lax.dot_general(
         g_all, out_weight, (((1,), (1,)), ((), ())), preferred_element_type=jnp.float32
     ).astype(jnp.bfloat16)
-    a_all = lax.all_to_all(a, "seq", split_axis=1, concat_axis=0, tiled=True)
-    d = lax.all_to_all(d_all, "seq", split_axis=0, concat_axis=1, tiled=True)
-
-    wo_grad = lax.dot_general(
-        a_all, g_all, (((0,), (0,)), ((), ())), preferred_element_type=jnp.float32
-    ).astype(jnp.bfloat16)
-    weight_grad = lax.psum_scatter(wo_grad, "dp", scatter_dimension=1, tiled=True)
+    a_all, d_all = lax.optimization_barrier((a_all, d_all))
+
+    mine = lax.axis_index("dp")
+    bit_lists = bit_orders(n_dp)
+    orders = [mine ^ jnp.asarray(offsets(bits), jnp.int32) for bits in bit_lists]
+    half = n_dp // 2
+    parts = range(len(bit_lists))
+    count = len(parts)
+    sent = [weight_blocks(a_all, g_all, orders[i][half:], i, count, n_dp) for i in parts]
+    kept = [weight_blocks(a_all, g_all, orders[i][:half], i, count, n_dp) for i in parts]
     product = jnp.dot(a_all, out_weight, preferred_element_type=jnp.float32)
-    y = lax.psum_scatter(product.astype(jnp.bfloat16), "seq", scatter_dimension=0, tiled=True)
+    product = product.astype(jnp.bfloat16)
+    y = lax.psum_scatter(product, "seq", scatter_dimension=0, tiled=True)
+
+    d = None
+    for level in range(len(bit_lists[0])):
+        totals = [exchange(sent[i], kept[i], bit_lists[i][level], n_dp) for i in parts]
+        if level == len(bit_lists[0]) - 1:
+            break
+        pairs = [split_half(total) for total in totals]
+        sent, kept = [pair[0] for pair in pairs], [pair[1] for pair in pairs]
+        if level == 0:
+            q, sent = lax.optimization_barrier((q, sent))
+            d = lax.all_to_all(d_all, "seq", split_axis=0, concat_axis=1, tiled=True)
+    weight_grad = jnp.concatenate([total[0] for total in totals], axis=0)
 
     k_out = pl.BlockSpec((wide, HEAD_SIZE), lambda i: (0, i))
     dq, dk, dv = pl.pallas_call(
@@ -162,7 +236,7 @@
         dq[None],
         total[None, :, :kvw],
         total[None, :, kvw:],
-        weight_grad.astype(jnp.float32),
+        weight_grad,
     )
 
 

time: 183 us -> 144 us (0.79)
  blocking collectives: 42.2 us -> 0 us
  waiting for transfers between devices: 84.8 us -> 43.3 us
  starting transfers between devices: 3.8 us -> 27 us
  local copies, waits for them, and re-layouts: 2.57 us -> 14 us
  Pallas kernels: 11.9 us -> 22.8 us
  matrix products: 18 us -> 12 us
  other arithmetic: 5.53 us -> 9.88 us
    reduce_scatter x2 -> x1, waiting for transfers between devices: 81.3 us -> 0.01 us  [local(): y = lax.psum_scatter(product, 'seq', scatter_dimension=0, tiled=True)]
    all_to_all x2 -> x0, blocking collectives: 42.2 us -> none  [the longest x1 25.2 us: local(): a_all = lax.all_to_all(a, 'seq', split_axis=1, concat_axis=0, tiled=True)]
    ppermute x0 -> x6, waiting for transfers between devices: none -> 32 us  [exchange(): got = lax.ppermute(sent, 'dp', [(i, i ^ bit) for i in range(n_dp)])]
    all_to_all x0 -> x2, starting transfers between devices: none -> 15.1 us  [the longest x1 10.8 us: local(): a_all = lax.all_to_all(a, 'seq', split_axis=1, concat_axis=0, tiled=True)]
    pallas_call x0 -> x4, Pallas kernels: none -> 10.9 us  [weight_blocks(): pl.pallas_call(weight_kernel, grid_spec=pltpu.PrefetchScalarGridSpec(num_...]
    all_to_all x0 -> x2, waiting for transfers between devices: none -> 8.75 us  [the longest x1 6.64 us: local(): a_all = lax.all_to_all(a, 'seq', split_axis=1, concat_axis=0, tiled=True)]
    ppermute x0 -> x6, starting transfers between devices: none -> 8.12 us  [exchange(): got = lax.ppermute(sent, 'dp', [(i, i ^ bit) for i in range(n_dp)])]
    unnamed x7 -> x33, local copies, waits for them, and re-layouts: 1.38 us -> 8.47 us
  transfers between devices with their start and end apart: 5 -> 12, of which waited for: 4 -> 8; matrix products, arithmetic and copies ran while one was open for 10% -> 15% of each run, Pallas kernels for 7% -> 16%
where the time goes in v2:
time: 144 us; the launch traced here: 143 us
  waiting for transfers between devices  43.3 us (30%)
  starting transfers between devices  27 us (19%)
  Pallas kernels  22.8 us (16%)
  between operations  14.3 us (10%)
  local copies, waits for them, and re-layouts  14 us (10%)
  matrix products  12 us (8%)
  other arithmetic  9.88 us (7%)
    ppermute x6, waiting for transfers between devices, exchange(): got = lax.ppermute(sent, 'dp', [(i, i ^ bit) for i in range(n_dp)])  32 us
    pallas_call x4, Pallas kernels, weight_blocks(): pl.pallas_call(weight_kernel, grid_spec=pltpu.PrefetchScalarGridSpec(num_...  10.9 us
    all_to_all x1, starting transfers between devices, local(): a_all = lax.all_to_all(a, 'seq', split_axis=1, concat_axis=0, tiled=True)  10.8 us
    unnamed x33, local copies, waits for them, and re-layouts  8.47 us
    ppermute x6, starting transfers between devices, exchange(): got = lax.ppermute(sent, 'dp', [(i, i ^ bit) for i in range(n_dp)])  8.12 us
    all_to_all x1, waiting for transfers between devices, local(): a_all = lax.all_to_all(a, 'seq', split_axis=1, concat_axis=0, tiled=True)  6.64 us
    dot_general x1, matrix products, local(): lax.dot_general(g_all, out_weight, (((1,), (1,)), ((), ())), preferred_el...  6.15 us
    pallas_call x1, Pallas kernels, local(): pl.pallas_call(backward_kernel, grid=(KEY_VALUE_HEADS,), in_specs=[q_spec...  6.09 us
  transfers between devices with their start and end apart: 12, of which 8 were waited for; matrix products, arithmetic and copies ran while one was open for 15% of the time, Pallas kernels for 16%

profile of v2, /device:TPU:0, one launch (start us, length us, event | category | flops | bytes accessed | tf_op | source)
XLA Modules:
  0.0 143.3 jit_solution(16634737815426150151)
XLA Ops:
  7.2 0.0 copy-start.4
  7.2 0.0 all-gather.3.cloned.1.call-start
  7.2 0.7 all-gather.3.cloned.1.call-update
  7.9 1.1 pad_maximum_fusion.1
  9.0 2.4 %collective-permute-start = (bf16[128,2048]{1,0:T(8,128)(2,1)S(1)}, bf16[128,2048]{1,0:T(8,128)(2,1)S(1)}, u32[]{:S(2)}, u32[]{:S(2)}) collective-permute-start(bf16[128,2048]{1,0:T(8,128)(2,1)S(1)} %pad_maximum_fusion.1), channel_id=1, source_target_pairs={{0,8},{8,16},{16,24},{1,9},{9,17},{17,25},{2,10},{10,18},{18,26},{... | collective-permute-start | bytes 1572872 | tf_op jit(solution)/shard_map/ppermute | solution.py:155
  11.4 0.9 select_reduce_fusion.2
  12.2 0.1 select_reduce_fusion.1
  12.4 0.1 select_reduce_fusion
  12.4 0.1 subtract_bitcast_fusion
  12.5 0.1 copy.20.first_ref
  12.6 0.2 collective-permute-done
  12.9 1.1 maximum_maximum_fusion.k_ref.v_ref
  14.0 5.8 %attention_forward.1 = (bf16[128,4096]{1,0:T(8,128)(2,1)S(1)}, bf16[8,512,256]{2,1,0:T(8,128)(2,1)S(1)}) custom-call(bf16[128,4096]{1,0:T(8,128)(2,1)S(1)} %bitcast.43, bf16[256,2048]{1,0:T(8,128)(2,1)S(1)} %maximum_maximum_fusion.k_ref.v_ref, bf16[256,2048]{1,0:T(8,128)(2,1)S(1)} %maximum_maximum_fusion.k_ref.v_ref, s32[128,1]{1,0:T(8,128)S(1)} %copy.20.first_ref), custom_call_target="tpu_custom_call" | custom-call | tf_op jit(solution)/shard_map/attention_forward/pallas_call | solution.py:167
  19.8 1.3 copy-done.8
  21.1 1.2 copy.26
  22.3 0.1 copy-done.6
  22.4 10.8 %all-to-all-start = ((bf16[128,4,1024]{2,0,1:T(8,128)(2,1)}), bf16[128,4,1024]{2,0,1:T(8,128)(2,1)S(1)}, u32[]{:S(2)}, u32[]{:S(2)}) async-start(bf16[128,4,1024]{2,0,1:T(8,128)(2,1)} %bitcast.47), calls=%async_computation | async-start | bytes 2097152 | tf_op jit(solution)/shard_map/all_to_all | solution.py:180
  33.2 1.7 %all-gather.3.cloned.1.call-done = bf16[1,512,2048]{2,1,0:T(8,128)(2,1)} async-done(((bf16[1,128,2048]{2,1,0:T(8,128)(2,1)}), bf16[1,512,2048]{2,1,0:T(8,128)(2,1)}) %all-gather.3.cloned.1.call-update) | async-done | bytes 2097168 | tf_op jit(solution)/shard_map/all_gather | solution.py:158
  34.9 6.1 %convolution_convert_fusion.1 = bf16[512,1024]{1,0:T(8,128)(2,1)} fusion(bf16[1024,2048]{1,0:T(8,128)(2,1)} %param.12, bf16[1,512,2048]{2,1,0:T(8,128)(2,1)} %all-gather.3.cloned.1.call-done), kind=kOutput, calls=%fused_computation.3 | convolution fusion | flops 2148007936 | bytes 7340032 | tf_op jit(solution)/shard_map/dot_general | solution.py:181
  41.0 6.6 %all-to-all-done = bf16[128,4,1024]{2,0,1:T(8,128)(2,1)S(1)} async-done(((bf16[128,4,1024]{2,0,1:T(8,128)(2,1)}), bf16[128,4,1024]{2,0,1:T(8,128)(2,1)S(1)}, u32[]{:S(2)}, u32[]{:S(2)}) %all-to-all-start) | async-done | bytes 1048608 | tf_op jit(solution)/shard_map/all_to_all | solution.py:180
  47.7 5.9 %convolution_convert_fusion = bf16[512,2048]{1,0:T(8,128)(2,1)} fusion(bf16[512,1024]{1,0:T(8,128)(2,1)S(1)} %bitcast.38, bf16[1024,2048]{1,0:T(8,128)(2,1)} %param.12), kind=kOutput, calls=%fused_computation | convolution fusion | flops 2148532224 | bytes 7340032 | tf_op jit(solution)/shard_map/dot_general | solution.py:194
  53.5 1.0 copy-done.1
  54.5 0.0 reduce-scatter.2.cloned.1.call-update
  54.5 0.1 fusion.1
  54.6 1.5 %copy-done = bf16[1,512,2048]{2,1,0:T(8,128)(2,1)S(1)} copy-done((bf16[1,512,2048]{2,1,0:T(8,128)(2,1)S(1)}, bf16[1,512,2048]{2,1,0:T(8,128)(2,1)}, u32[]{:S(2)}) %copy-start) | copy-done | bytes 2097176
  56.1 1.2 copy-done.2
  57.3 3.2 %weight_blocks.7 = bf16[4,512,256]{2,1,0:T(8,128)(2,1)} custom-call(s32[4]{0:T(128)S(1)} %get-tuple-element.28.order_ref, bf16[512,1024]{1,0:T(8,128)(2,1)S(1)} %bitcast.39, bf16[512,2048]{1,0:T(8,128)(2,1)S(1)} %bitcast.34), custom_call_target="tpu_custom_call" | custom-call | flops 536870912 | bytes 2621440 | tf_op jit(solution)/shard_map/weight_blocks/pallas_call | solution.py:99
  60.6 1.6 %collective-permute-start.2 = (bf16[4,512,256]{2,1,0:T(8,128)(2,1)}, bf16[4,512,256]{2,1,0:T(8,128)(2,1)}, u32[]{:S(2)}, u32[]{:S(2)}) collective-permute-start(bf16[4,512,256]{2,1,0:T(8,128)(2,1)} %weight_blocks.7), channel_id=1, source_target_pairs={{0,2},{1,3},{2,0},{3,1},{4,6},{5,7},{6,4},{7,5},{8,10},{9,11},{10,... | collective-permute-start | bytes 3145736 | tf_op jit(solution)/shard_map/ppermute | solution.py:119
  62.2 0.1 fusion.2
  62.2 3.2 %weight_blocks.5 = bf16[4,512,256]{2,1,0:T(8,128)(2,1)} custom-call(s32[4]{0:T(128)S(1)} %get-tuple-element.30.order_ref, bf16[512,1024]{1,0:T(8,128)(2,1)S(1)} %bitcast.40, bf16[512,2048]{1,0:T(8,128)(2,1)S(1)} %bitcast.35), custom_call_target="tpu_custom_call" | custom-call | flops 536870912 | bytes 2621440 | tf_op jit(solution)/shard_map/weight_blocks/pallas_call | solution.py:99
  65.5 1.5 %collective-permute-start.1 = (bf16[4,512,256]{2,1,0:T(8,128)(2,1)}, bf16[4,512,256]{2,1,0:T(8,128)(2,1)}, u32[]{:S(2)}, u32[]{:S(2)}) collective-permute-start(bf16[4,512,256]{2,1,0:T(8,128)(2,1)} %weight_blocks.5), channel_id=1, source_target_pairs={{0,1},{1,0},{2,3},{3,2},{4,5},{5,4},{6,7},{7,6},{8,9},{9,8},{10,11... | collective-permute-start | bytes 3145736 | tf_op jit(solution)/shard_map/ppermute | solution.py:119
  67.0 4.2 %all-to-all-start.1 = ((bf16[4,128,1024]{2,1,0:T(8,128)(2,1)}), bf16[4,128,1024]{2,1,0:T(8,128)(2,1)}, u32[]{:S(2)}, u32[]{:S(2)}) async-start(bf16[4,128,1024]{2,1,0:T(8,128)(2,1)} %bitcast.48), calls=%async_computation.2 | async-start | bytes 2097152 | tf_op jit(solution)/shard_map/all_to_all | solution.py:207
  71.2 0.0 copy-start.3
  71.2 1.4 copy-done.3
  72.7 2.2 %weight_blocks.6 = bf16[4,512,256]{2,1,0:T(8,128)(2,1)S(1)} custom-call(s32[4]{0:T(128)S(1)} %get-tuple-element.27.order_ref, bf16[512,1024]{1,0:T(8,128)(2,1)S(1)} %bitcast.41, bf16[512,2048]{1,0:T(8,128)(2,1)S(1)} %bitcast.36), custom_call_target="tpu_custom_call" | custom-call | flops 536870912 | bytes 2621440 | tf_op jit(solution)/shard_map/weight_blocks/pallas_call | solution.py:99
  74.9 2.2 %weight_blocks.4 = bf16[4,512,256]{2,1,0:T(8,128)(2,1)S(1)} custom-call(s32[4]{0:T(128)S(1)} %get-tuple-element.29.order_ref, bf16[512,1024]{1,0:T(8,128)(2,1)S(1)} %bitcast.42, bf16[512,2048]{1,0:T(8,128)(2,1)S(1)} %bitcast.37), custom_call_target="tpu_custom_call" | custom-call | flops 536870912 | bytes 2621440 | tf_op jit(solution)/shard_map/weight_blocks/pallas_call | solution.py:99
  77.1 8.2 %collective-permute-done.2 = bf16[4,512,256]{2,1,0:T(8,128)(2,1)} collective-permute-done((bf16[4,512,256]{2,1,0:T(8,128)(2,1)}, bf16[4,512,256]{2,1,0:T(8,128)(2,1)}, u32[]{:S(2)}, u32[]{:S(2)}) %collective-permute-start.2) | collective-permute-done | bytes 1048608 | tf_op jit(solution)/shard_map/ppermute | solution.py:119
  85.4 1.5 %add_convert_fusion = bf16[4,512,256]{2,1,0:T(8,128)(2,1)S(1)} fusion(bf16[4,512,256]{2,1,0:T(8,128)(2,1)} %collective-permute-done.2, bf16[4,512,256]{2,1,0:T(8,128)(2,1)S(1)} %weight_blocks.6), kind=kLoop, calls=%fused_computation.1 | loop fusion | flops 2097152 | bytes 3145728 | tf_op jit(solution)/shard_map/convert_element_type | solution.py:124
  86.8 0.0 copy-start.10
  86.8 1.0 slice.65
  87.8 2.2 %collective-permute-done.1 = bf16[4,512,256]{2,1,0:T(8,128)(2,1)} collective-permute-done((bf16[4,512,256]{2,1,0:T(8,128)(2,1)}, bf16[4,512,256]{2,1,0:T(8,128)(2,1)}, u32[]{:S(2)}, u32[]{:S(2)}) %collective-permute-start.1) | collective-permute-done | bytes 1048608 | tf_op jit(solution)/shard_map/ppermute | solution.py:119
  90.0 1.5 %add_convert_fusion.1 = bf16[4,512,256]{2,1,0:T(8,128)(2,1)S(1)} fusion(bf16[4,512,256]{2,1,0:T(8,128)(2,1)} %collective-permute-done.1, bf16[4,512,256]{2,1,0:T(8,128)(2,1)S(1)} %weight_blocks.4), kind=kLoop, calls=%fused_computation.2 | loop fusion | flops 2097152 | bytes 3145728 | tf_op jit(solution)/shard_map/convert_element_type | solution.py:124
  91.5 0.0 copy-start.7
  91.5 0.8 slice.64
  92.3 0.3 copy-done.12
  92.6 0.4 collective-permute-start.4
  93.0 1.5 %collective-permute-start.6 = (bf16[2,512,256]{2,1,0:T(8,128)(2,1)}, bf16[2,512,256]{2,1,0:T(8,128)(2,1)}, u32[]{:S(2)}, u32[]{:S(2)}) collective-permute-start(bf16[2,512,256]{2,1,0:T(8,128)(2,1)} %slice.65), channel_id=1, source_target_pairs={{0,1},{1,0},{2,3},{3,2},{4,5},{5,4},{6,7},{7,6},{8,9},{9,8},{10,11... | collective-permute-start | bytes 1572872 | tf_op jit(solution)/shard_map/ppermute | solution.py:119
  94.5 2.1 %all-to-all-done.1 = bf16[4,128,1024]{2,1,0:T(8,128)(2,1)} async-done(((bf16[4,128,1024]{2,1,0:T(8,128)(2,1)}), bf16[4,128,1024]{2,1,0:T(8,128)(2,1)}, u32[]{:S(2)}, u32[]{:S(2)}) %all-to-all-start.1) | async-done | bytes 1048608 | tf_op jit(solution)/shard_map/all_to_all | solution.py:207
  96.7 1.3 copy.24
  98.0 1.6 %copy-done.9 = bf16[8,512,256]{2,1,0:T(8,128)(2,1)S(1)} copy-done((bf16[8,512,256]{2,1,0:T(8,128)(2,1)S(1)}, bf16[8,512,256]{2,1,0:T(8,128)(2,1)}, u32[]{:S(2)}) %copy-start.9) | copy-done | bytes 2097176
  99.6 6.1 %attention_backward.1 = (bf16[128,4096]{1,0:T(8,128)(2,1)}, bf16[256,1024]{1,0:T(8,128)(2,1)S(1)}, bf16[256,1024]{1,0:T(8,128)(2,1)S(1)}) custom-call(bf16[128,4096]{1,0:T(8,128)(2,1)S(1)} %bitcast.44, bf16[256,2048]{1,0:T(8,128)(2,1)S(1)} %maximum_maximum_fusion.k_ref.v_ref, bf16[256,2048]{1,0:T(8,128)(2,1)S(1)} %maximum_maximum_fusion.k_ref.v_ref, ...), custom_call_target="tpu_custom_call" | custom-call | tf_op jit(solution)/shard_map/attention_backward/pallas_call | solution.py:211
  105.7 0.0 copy-start.11
  105.9 1.4 collective-permute-start.3
  107.3 1.2 add_convert_fusion.3
  108.5 2.5 %collective-permute-start.5 = (bf16[1,512,256]{2,1,0:T(8,128)(2,1)S(1)}, bf16[1,512,256]{2,1,0:T(8,128)(2,1)S(1)}, u32[]{:S(2)}, u32[]{:S(2)}) collective-permute-start(bf16[1,512,256]{2,1,0:T(8,128)(2,1)S(1)} %slice.72), channel_id=1, source_target_pairs={{0,4},{1,5},{2,6},{3,7},{4,0},{5,1},{6,2},{7,3},{8,12},{9,13},{10,... | collective-permute-start | bytes 786440 | tf_op jit(solution)/shard_map/ppermute | solution.py:119
  111.0 1.2 add_convert_fusion.2
  112.2 0.6 collective-permute-start.7
  112.8 0.1 add_convert_fusion.4
  112.9 0.8 slice_bitcast_fusion
  113.7 16.0 %collective-permute-done.5 = bf16[1,512,256]{2,1,0:T(8,128)(2,1)S(1)} collective-permute-done((bf16[1,512,256]{2,1,0:T(8,128)(2,1)S(1)}, bf16[1,512,256]{2,1,0:T(8,128)(2,1)S(1)}, u32[]{:S(2)}, u32[]{:S(2)}) %collective-permute-start.5) | collective-permute-done | bytes 262176 | tf_op jit(solution)/shard_map/ppermute | solution.py:119
  129.8 0.1 add_bitcast_fusion.1
  129.8 5.6 %collective-permute-done.7 = bf16[1,512,256]{2,1,0:T(8,128)(2,1)S(1)} collective-permute-done((bf16[1,512,256]{2,1,0:T(8,128)(2,1)S(1)}, bf16[1,512,256]{2,1,0:T(8,128)(2,1)S(1)}, u32[]{:S(2)}, u32[]{:S(2)}) %collective-permute-start.7) | collective-permute-done | bytes 262176 | tf_op jit(solution)/shard_map/ppermute | solution.py:119
  135.4 0.1 add_bitcast_fusion
  135.4 1.0 pad_maximum_fusion
  (30 shorter events, 0.2 us)
Async XLA Ops:
  7.2 6.8 %copy-start.4 = (bf16[1,128,4096]{2,1,0:T(8,128)(2,1)S(1)}, bf16[1,128,4096]{2,1,0:T(8,128)(2,1)}, u32[]{:S(2)}) copy-start(bf16[1,128,4096]{2,1,0:T(8,128)(2,1)} %param.9) | copy-start | bytes 3145732
  7.2 27.7 %all-gather.3.cloned.1.call-start = ((), (), s32[]{:S(2)}) async-start(), calls=%async_computation.4 | async-start | bytes 2621440 | tf_op jit(solution)/shard_map/all_gather | solution.py:158
  9.0 3.9 %collective-permute-start = (bf16[128,2048]{1,0:T(8,128)(2,1)S(1)}, bf16[128,2048]{1,0:T(8,128)(2,1)S(1)}, u32[]{:S(2)}, u32[]{:S(2)}) collective-permute-start(bf16[128,2048]{1,0:T(8,128)(2,1)S(1)} %pad_maximum_fusion.1), channel_id=1, source_target_pairs={{0,8},{8,16},{16,24},{1,9},{9,17},{17,25},{2,10},{10,18},{18,26},{... | collective-permute-start | bytes 1572872 | tf_op jit(solution)/shard_map/ppermute | solution.py:155
  19.8 1.3 copy-start.8
  21.1 1.3 copy-start.6
  21.1 12.1 %copy-start.14 = (s32[8]{0:T(128)S(1)}, s32[8]{0:T(128)}, u32[]{:S(2)}) copy-start(s32[8]{0:T(128)} %constant.21.clone) | copy-start | bytes 100
  21.1 12.1 %copy-start.15 = (s32[8]{0:T(128)S(1)}, s32[8]{0:T(128)}, u32[]{:S(2)}) copy-start(s32[8]{0:T(128)} %constant.22.clone) | copy-start | bytes 100
  22.4 25.3 %all-to-all-start = ((bf16[128,4,1024]{2,0,1:T(8,128)(2,1)}), bf16[128,4,1024]{2,0,1:T(8,128)(2,1)S(1)}, u32[]{:S(2)}, u32[]{:S(2)}) async-start(bf16[128,4,1024]{2,0,1:T(8,128)(2,1)} %bitcast.47), calls=%async_computation | async-start | bytes 2097152 | tf_op jit(solution)/shard_map/all_to_all | solution.py:180
  33.2 103.3 %reduce-scatter.2.cloned.1.call-start = ((), (), s32[]{:S(2)}) async-start(), calls=%async_computation.3 | async-start | bytes 2621440 | tf_op jit(solution)/shard_map/reduce_scatter | solution.py:196
  53.5 1.0 copy-start.1
  54.5 1.6 %copy-start = (bf16[1,512,2048]{2,1,0:T(8,128)(2,1)S(1)}, bf16[1,512,2048]{2,1,0:T(8,128)(2,1)}, u32[]{:S(2)}) copy-start(bf16[1,512,2048]{2,1,0:T(8,128)(2,1)} %all-gather.3.cloned.1.call-done) | copy-start | bytes 6291460
  56.1 1.2 copy-start.2
  60.6 24.8 %collective-permute-start.2 = (bf16[4,512,256]{2,1,0:T(8,128)(2,1)}, bf16[4,512,256]{2,1,0:T(8,128)(2,1)}, u32[]{:S(2)}, u32[]{:S(2)}) collective-permute-start(bf16[4,512,256]{2,1,0:T(8,128)(2,1)} %weight_blocks.7), channel_id=1, source_target_pairs={{0,2},{1,3},{2,0},{3,1},{4,6},{5,7},{6,4},{7,5},{8,10},{9,11},{10,... | collective-permute-start | bytes 3145736 | tf_op jit(solution)/shard_map/ppermute | solution.py:119
  65.5 24.5 %collective-permute-start.1 = (bf16[4,512,256]{2,1,0:T(8,128)(2,1)}, bf16[4,512,256]{2,1,0:T(8,128)(2,1)}, u32[]{:S(2)}, u32[]{:S(2)}) collective-permute-start(bf16[4,512,256]{2,1,0:T(8,128)(2,1)} %weight_blocks.5), channel_id=1, source_target_pairs={{0,1},{1,0},{2,3},{3,2},{4,5},{5,4},{6,7},{7,6},{8,9},{9,8},{10,11... | collective-permute-start | bytes 3145736 | tf_op jit(solution)/shard_map/ppermute | solution.py:119
  67.0 29.7 %all-to-all-start.1 = ((bf16[4,128,1024]{2,1,0:T(8,128)(2,1)}), bf16[4,128,1024]{2,1,0:T(8,128)(2,1)}, u32[]{:S(2)}, u32[]{:S(2)}) async-start(bf16[4,128,1024]{2,1,0:T(8,128)(2,1)} %bitcast.48), calls=%async_computation.2 | async-start | bytes 2097152 | tf_op jit(solution)/shard_map/all_to_all | solution.py:207
  71.2 1.4 %copy-start.3 = (bf16[128,4,1024]{2,0,1:T(8,128)(2,1)S(1)}, bf16[128,4,1024]{2,0,1:T(8,128)(2,1)}, u32[]{:S(2)}) copy-start(bf16[128,4,1024]{2,0,1:T(8,128)(2,1)} %copy-done.1) | copy-start | bytes 3145732
  86.8 4.6 %copy-start.10 = (bf16[4,512,256]{2,1,0:T(8,128)(2,1)}, bf16[4,512,256]{2,1,0:T(8,128)(2,1)S(1)}, u32[]{:S(2)}) copy-start(bf16[4,512,256]{2,1,0:T(8,128)(2,1)S(1)} %add_convert_fusion) | copy-start | bytes 3145732
  91.4 1.1 copy-start.12
  91.4 6.6 %copy-start.5 = (bf16[1,128,4096]{2,1,0:T(8,128)(2,1)S(1)}, bf16[1,128,4096]{2,1,0:T(8,128)(2,1)}, u32[]{:S(2)}) copy-start(bf16[1,128,4096]{2,1,0:T(8,128)(2,1)} %param.9) | copy-start | bytes 3145732
  91.5 6.6 %copy-start.7 = (bf16[128,4096]{1,0:T(8,128)(2,1)S(1)}, bf16[128,4096]{1,0:T(8,128)(2,1)}, u32[]{:S(2)}) copy-start(bf16[128,4096]{1,0:T(8,128)(2,1)} %copy-done.6) | copy-start | bytes 3145732
  92.6 14.7 %collective-permute-start.4 = (bf16[2,512,256]{2,1,0:T(8,128)(2,1)}, bf16[2,512,256]{2,1,0:T(8,128)(2,1)}, u32[]{:S(2)}, u32[]{:S(2)}) collective-permute-start(bf16[2,512,256]{2,1,0:T(8,128)(2,1)} %slice.64), channel_id=1, source_target_pairs={{0,2},{1,3},{2,0},{3,1},{4,6},{5,7},{6,4},{7,5},{8,10},{9,11},{10,... | collective-permute-start | bytes 1572872 | tf_op jit(solution)/shard_map/ppermute | solution.py:119
  93.0 18.0 %collective-permute-start.6 = (bf16[2,512,256]{2,1,0:T(8,128)(2,1)}, bf16[2,512,256]{2,1,0:T(8,128)(2,1)}, u32[]{:S(2)}, u32[]{:S(2)}) collective-permute-start(bf16[2,512,256]{2,1,0:T(8,128)(2,1)} %slice.65), channel_id=1, source_target_pairs={{0,1},{1,0},{2,3},{3,2},{4,5},{5,4},{6,7},{7,6},{8,9},{9,8},{10,11... | collective-permute-start | bytes 1572872 | tf_op jit(solution)/shard_map/ppermute | solution.py:119
  98.0 1.6 %copy-start.9 = (bf16[8,512,256]{2,1,0:T(8,128)(2,1)S(1)}, bf16[8,512,256]{2,1,0:T(8,128)(2,1)}, u32[]{:S(2)}) copy-start(bf16[8,512,256]{2,1,0:T(8,128)(2,1)} %copy-done.8) | copy-start | bytes 6291460
  105.7 1.6 %copy-start.13 = (bf16[4,512,256]{2,1,0:T(8,128)(2,1)S(1)}, bf16[4,512,256]{2,1,0:T(8,128)(2,1)}, u32[]{:S(2)}) copy-start(bf16[4,512,256]{2,1,0:T(8,128)(2,1)} %copy-done.12) | copy-start | bytes 3145732
  105.7 5.2 %copy-start.11 = (bf16[4,512,256]{2,1,0:T(8,128)(2,1)S(1)}, bf16[4,512,256]{2,1,0:T(8,128)(2,1)}, u32[]{:S(2)}) copy-start(bf16[4,512,256]{2,1,0:T(8,128)(2,1)} %copy-done.10) | copy-start | bytes 3145732
  105.9 6.9 %collective-permute-start.3 = (bf16[128,2048]{1,0:T(8,128)(2,1)S(1)}, bf16[128,2048]{1,0:T(8,128)(2,1)S(1)}, u32[]{:S(2)}, u32[]{:S(2)}) collective-permute-start(bf16[128,2048]{1,0:T(8,128)(2,1)S(1)} %slice.67), channel_id=1, source_target_pairs={{8,0},{16,8},{24,16},{9,1},{17,9},{25,17},{10,2},{18,10},{26,18},{... | collective-permute-start | bytes 1572872 | tf_op jit(solution)/shard_map/ppermute | solution.py:227
  108.5 21.3 %collective-permute-start.5 = (bf16[1,512,256]{2,1,0:T(8,128)(2,1)S(1)}, bf16[1,512,256]{2,1,0:T(8,128)(2,1)S(1)}, u32[]{:S(2)}, u32[]{:S(2)}) collective-permute-start(bf16[1,512,256]{2,1,0:T(8,128)(2,1)S(1)} %slice.72), channel_id=1, source_target_pairs={{0,4},{1,5},{2,6},{3,7},{4,0},{5,1},{6,2},{7,3},{8,12},{9,13},{10,... | collective-permute-start | bytes 786440 | tf_op jit(solution)/shard_map/ppermute | solution.py:119
  112.2 23.2 %collective-permute-start.7 = (bf16[1,512,256]{2,1,0:T(8,128)(2,1)S(1)}, bf16[1,512,256]{2,1,0:T(8,128)(2,1)S(1)}, u32[]{:S(2)}, u32[]{:S(2)}) collective-permute-start(bf16[1,512,256]{2,1,0:T(8,128)(2,1)S(1)} %slice.75), channel_id=1, source_target_pairs={{0,4},{1,5},{2,6},{3,7},{4,0},{5,1},{6,2},{7,3},{8,12},{9,13},{10,... | collective-permute-start | bytes 786440 | tf_op jit(solution)/shard_map/ppermute | solution.py:119
Sparse Core Ops, SparseCore 0:
  9.6 25.2 all-gather.2
  54.7 42.9 reduce-scatter.1

commit v3 on v2

--- a/solution.py
+++ b/solution.py
@@ -191,6 +191,7 @@
     count = len(parts)
     sent = [weight_blocks(a_all, g_all, orders[i][half:], i, count, n_dp) for i in parts]
     kept = [weight_blocks(a_all, g_all, orders[i][:half], i, count, n_dp) for i in parts]
+    a_all, sent[0] = lax.optimization_barrier((a_all, sent[0]))
     product = jnp.dot(a_all, out_weight, preferred_element_type=jnp.float32)
     product = product.astype(jnp.bfloat16)
     y = lax.psum_scatter(product, "seq", scatter_dimension=0, tiled=True)

time: 144 us -> 140 us (0.972)
  waiting for transfers between devices: 43.3 us -> 39.3 us
  local copies, waits for them, and re-layouts: 14 us -> 10.8 us
  Pallas kernels: 22.8 us -> 25.8 us
    unnamed x33 -> x27, local copies, waits for them, and re-layouts: 8.47 us -> 5.31 us
    pallas_call x4, Pallas kernels: 10.9 us -> 13.9 us  [weight_blocks(): pl.pallas_call(weight_kernel, grid_spec=pltpu.PrefetchScalarGridSpec(num_...]
    all_to_all x1, waiting for transfers between devices: 2.12 us -> 0.01 us  [local(): d = lax.all_to_all(d_all, 'seq', split_axis=0, concat_axis=1, tiled=True)]
    ppermute x6, waiting for transfers between devices: 32 us -> 30.4 us  [exchange(): got = lax.ppermute(sent, 'dp', [(i, i ^ bit) for i in range(n_dp)])]
  transfers between devices with their start and end apart: 12 -> 12, of which waited for: 8 -> 6; matrix products, arithmetic and copies ran while one was open for 15% -> 16% of each run, Pallas kernels for 16% -> 16%
where the time goes in v3:
time: 140 us; the launch traced here: 139 us
  waiting for transfers between devices  39.3 us (28%)
  starting transfers between devices  26.8 us (19%)
  Pallas kernels  25.8 us (18%)
  between operations  14.3 us (10%)
  matrix products  11.2 us (8%)
  local copies, waits for them, and re-layouts  10.8 us (8%)
  other arithmetic  10.6 us (8%)
    ppermute x6, waiting for transfers between devices, exchange(): got = lax.ppermute(sent, 'dp', [(i, i ^ bit) for i in range(n_dp)])  30.4 us
    pallas_call x4, Pallas kernels, weight_blocks(): pl.pallas_call(weight_kernel, grid_spec=pltpu.PrefetchScalarGridSpec(num_...  13.9 us
    all_to_all x1, starting transfers between devices, local(): a_all = lax.all_to_all(a, 'seq', split_axis=1, concat_axis=0, tiled=True)  10.4 us
    ppermute x6, starting transfers between devices, exchange(): got = lax.ppermute(sent, 'dp', [(i, i ^ bit) for i in range(n_dp)])  8.3 us
    all_to_all x1, waiting for transfers between devices, local(): a_all = lax.all_to_all(a, 'seq', split_axis=1, concat_axis=0, tiled=True)  6.54 us
    dot_general x1, matrix products, local(): lax.dot_general(g_all, out_weight, (((1,), (1,)), ((), ())), preferred_el...  6.34 us
    pallas_call x1, Pallas kernels, local(): pl.pallas_call(backward_kernel, grid=(KEY_VALUE_HEADS,), in_specs=[q_spec...  6.09 us
    pallas_call x1, Pallas kernels, local(): pl.pallas_call(forward_kernel, grid=(KEY_VALUE_HEADS,), in_specs=[q_spec,...  5.77 us
  transfers between devices with their start and end apart: 12, of which 6 were waited for; matrix products, arithmetic and copies ran while one was open for 16% of the time, Pallas kernels for 16%

profile of v3, /device:TPU:0, one launch (start us, length us, event | category | flops | bytes accessed | tf_op | source)
XLA Modules:
  0.0 138.7 jit_solution(621607714932100215)
XLA Ops:
  7.2 0.0 copy-start.1
  7.2 0.0 all-gather.3.cloned.1.call-start
  7.2 0.7 all-gather.3.cloned.1.call-update
  7.9 1.1 pad_maximum_fusion.1
  9.0 2.4 %collective-permute-start = (bf16[128,2048]{1,0:T(8,128)(2,1)S(1)}, bf16[128,2048]{1,0:T(8,128)(2,1)S(1)}, u32[]{:S(2)}, u32[]{:S(2)}) collective-permute-start(bf16[128,2048]{1,0:T(8,128)(2,1)S(1)} %pad_maximum_fusion.1), channel_id=1, source_target_pairs={{0,8},{8,16},{16,24},{1,9},{9,17},{17,25},{2,10},{10,18},{18,26},{... | collective-permute-start | bytes 1572872 | tf_op jit(solution)/shard_map/ppermute | solution.py:155
  11.4 0.9 select_reduce_fusion.2
  12.2 0.1 select_reduce_fusion.1
  12.4 0.1 select_reduce_fusion
  12.4 0.1 subtract_bitcast_fusion
  12.5 0.1 copy.20.first_ref
  12.6 0.7 broadcast_xor_fusion
  13.3 0.0 collective-permute-done
  13.3 1.1 maximum_maximum_fusion.k_ref.v_ref
  14.5 5.8 %attention_forward.1 = (bf16[128,4096]{1,0:T(8,128)(2,1)S(1)}, bf16[8,512,256]{2,1,0:T(8,128)(2,1)S(1)}) custom-call(bf16[128,4096]{1,0:T(8,128)(2,1)S(1)} %bitcast.38, bf16[256,2048]{1,0:T(8,128)(2,1)S(1)} %maximum_maximum_fusion.k_ref.v_ref, bf16[256,2048]{1,0:T(8,128)(2,1)S(1)} %maximum_maximum_fusion.k_ref.v_ref, s32[128,1]{1,0:T(8,128)S(1)} %copy.20.first_ref), custom_call_target="tpu_custom_call" | custom-call | tf_op jit(solution)/shard_map/attention_forward/pallas_call | solution.py:167
  20.2 1.3 copy-done.5
  21.5 1.2 copy.26
  22.7 0.1 copy-done.3
  22.9 10.4 %all-to-all-start = ((bf16[128,4,1024]{2,0,1:T(8,128)(2,1)}), bf16[128,4,1024]{2,0,1:T(8,128)(2,1)}, u32[]{:S(2)}, u32[]{:S(2)}) async-start(bf16[128,4,1024]{2,0,1:T(8,128)(2,1)} %bitcast.33), calls=%async_computation | async-start | bytes 2097152 | tf_op jit(solution)/shard_map/all_to_all | solution.py:180
  33.2 0.1 fusion.2
  33.3 1.6 %all-gather.3.cloned.1.call-done = bf16[1,512,2048]{2,1,0:T(8,128)(2,1)} async-done(((bf16[1,128,2048]{2,1,0:T(8,128)(2,1)}), bf16[1,512,2048]{2,1,0:T(8,128)(2,1)}) %all-gather.3.cloned.1.call-update) | async-done | bytes 2097168 | tf_op jit(solution)/shard_map/all_gather | solution.py:158
  34.9 6.3 %convolution_convert_fusion.1 = bf16[512,1024]{1,0:T(8,128)(2,1)} fusion(bf16[1024,2048]{1,0:T(8,128)(2,1)} %param.12, bf16[1,512,2048]{2,1,0:T(8,128)(2,1)} %all-gather.3.cloned.1.call-done), kind=kOutput, calls=%fused_computation.3 | convolution fusion | flops 2148007936 | bytes 7340032 | tf_op jit(solution)/shard_map/dot_general | solution.py:181
  41.2 6.5 %all-to-all-done = bf16[128,4,1024]{2,0,1:T(8,128)(2,1)} async-done(((bf16[128,4,1024]{2,0,1:T(8,128)(2,1)}), bf16[128,4,1024]{2,0,1:T(8,128)(2,1)}, u32[]{:S(2)}, u32[]{:S(2)}) %all-to-all-start) | async-done | bytes 1048608 | tf_op jit(solution)/shard_map/all_to_all | solution.py:180
  47.8 3.5 %weight_blocks.4 = bf16[4,512,256]{2,1,0:T(8,128)(2,1)S(1)} custom-call(s32[4]{0:T(128)S(1)} %get-tuple-element.34.order_ref, bf16[512,1024]{1,0:T(8,128)(2,1)} %bitcast.7.a_ref, bf16[512,2048]{1,0:T(8,128)(2,1)S(1)} %bitcast.34), custom_call_target="tpu_custom_call" | custom-call | flops 536870912 | bytes 2621440 | tf_op jit(solution)/shard_map/weight_blocks/pallas_call | solution.py:99
  51.3 1.1 copy-done.7
  52.3 4.9 %convolution_convert_fusion = bf16[512,2048]{1,0:T(8,128)(2,1)} fusion(bf16[512,1024]{1,0:T(8,128)(2,1)} %bitcast.7.a_ref, bf16[1024,2048]{1,0:T(8,128)(2,1)S(1)} %copy-done.12), kind=kOutput, calls=%fused_computation | convolution fusion | flops 2148532224 | bytes 7340032 | tf_op jit(solution)/shard_map/dot_general | solution.py:195
  57.2 0.0 reduce-scatter.2.cloned.1.call-update
  57.2 1.6 %collective-permute-start.1 = (bf16[4,512,256]{2,1,0:T(8,128)(2,1)}, bf16[4,512,256]{2,1,0:T(8,128)(2,1)}, u32[]{:S(2)}, u32[]{:S(2)}) collective-permute-start(bf16[4,512,256]{2,1,0:T(8,128)(2,1)} %copy-done.7), channel_id=1, source_target_pairs={{0,1},{1,0},{2,3},{3,2},{4,5},{5,4},{6,7},{7,6},{8,9},{9,8},{10,11... | collective-permute-start | bytes 3145736 | tf_op jit(solution)/shard_map/ppermute | solution.py:119
  58.8 0.1 fusion.1
  58.9 4.2 %weight_blocks.7 = bf16[4,512,256]{2,1,0:T(8,128)(2,1)} custom-call(s32[4]{0:T(128)S(1)} %get-tuple-element.32.order_ref, bf16[512,1024]{1,0:T(8,128)(2,1)} %bitcast.7.a_ref, bf16[512,2048]{1,0:T(8,128)(2,1)S(1)} %bitcast.35), custom_call_target="tpu_custom_call" | custom-call | flops 536870912 | bytes 2621440 | tf_op jit(solution)/shard_map/weight_blocks/pallas_call | solution.py:99
  63.1 1.6 %collective-permute-start.2 = (bf16[4,512,256]{2,1,0:T(8,128)(2,1)}, bf16[4,512,256]{2,1,0:T(8,128)(2,1)}, u32[]{:S(2)}, u32[]{:S(2)}) collective-permute-start(bf16[4,512,256]{2,1,0:T(8,128)(2,1)} %weight_blocks.7), channel_id=1, source_target_pairs={{0,2},{1,3},{2,0},{3,1},{4,6},{5,7},{6,4},{7,5},{8,10},{9,11},{10,... | collective-permute-start | bytes 3145736 | tf_op jit(solution)/shard_map/ppermute | solution.py:119
  64.6 4.3 %all-to-all-start.1 = ((bf16[4,128,1024]{2,1,0:T(8,128)(2,1)}), bf16[4,128,1024]{2,1,0:T(8,128)(2,1)}, u32[]{:S(2)}, u32[]{:S(2)}) async-start(bf16[4,128,1024]{2,1,0:T(8,128)(2,1)} %bitcast.42), calls=%async_computation.2 | async-start | bytes 2097152 | tf_op jit(solution)/shard_map/all_to_all | solution.py:208
  68.9 3.2 %weight_blocks.5 = bf16[4,512,256]{2,1,0:T(8,128)(2,1)S(1)} custom-call(s32[4]{0:T(128)S(1)} %get-tuple-element.33.order_ref, bf16[512,1024]{1,0:T(8,128)(2,1)} %bitcast.7.a_ref, bf16[512,2048]{1,0:T(8,128)(2,1)S(1)} %bitcast.36), custom_call_target="tpu_custom_call" | custom-call | flops 536870912 | bytes 2621440 | tf_op jit(solution)/shard_map/weight_blocks/pallas_call | solution.py:99
  72.1 3.2 %weight_blocks.6 = bf16[4,512,256]{2,1,0:T(8,128)(2,1)S(1)} custom-call(s32[4]{0:T(128)S(1)} %get-tuple-element.31.order_ref, bf16[512,1024]{1,0:T(8,128)(2,1)} %bitcast.7.a_ref, bf16[512,2048]{1,0:T(8,128)(2,1)S(1)} %bitcast.37), custom_call_target="tpu_custom_call" | custom-call | flops 536870912 | bytes 2621440 | tf_op jit(solution)/shard_map/weight_blocks/pallas_call | solution.py:99
  75.2 6.0 %collective-permute-done.1 = bf16[4,512,256]{2,1,0:T(8,128)(2,1)} collective-permute-done((bf16[4,512,256]{2,1,0:T(8,128)(2,1)}, bf16[4,512,256]{2,1,0:T(8,128)(2,1)}, u32[]{:S(2)}, u32[]{:S(2)}) %collective-permute-start.1) | collective-permute-done | bytes 1048608 | tf_op jit(solution)/shard_map/ppermute | solution.py:119
  81.2 1.5 %add_convert_fusion.1 = bf16[4,512,256]{2,1,0:T(8,128)(2,1)S(1)} fusion(bf16[4,512,256]{2,1,0:T(8,128)(2,1)} %collective-permute-done.1, bf16[4,512,256]{2,1,0:T(8,128)(2,1)S(1)} %weight_blocks.5), kind=kLoop, calls=%fused_computation.2 | loop fusion | flops 2097152 | bytes 3145728 | tf_op jit(solution)/shard_map/convert_element_type | solution.py:124
  82.7 1.0 slice.64
  83.7 0.2 copy-done.10
  83.9 2.8 %collective-permute-done.2 = bf16[4,512,256]{2,1,0:T(8,128)(2,1)} collective-permute-done((bf16[4,512,256]{2,1,0:T(8,128)(2,1)}, bf16[4,512,256]{2,1,0:T(8,128)(2,1)}, u32[]{:S(2)}, u32[]{:S(2)}) %collective-permute-start.2) | collective-permute-done | bytes 1048608 | tf_op jit(solution)/shard_map/ppermute | solution.py:119
  86.7 1.5 %add_convert_fusion = bf16[4,512,256]{2,1,0:T(8,128)(2,1)S(1)} fusion(bf16[4,512,256]{2,1,0:T(8,128)(2,1)} %collective-permute-done.2, bf16[4,512,256]{2,1,0:T(8,128)(2,1)S(1)} %weight_blocks.6), kind=kLoop, calls=%fused_computation.1 | loop fusion | flops 2097152 | bytes 3145728 | tf_op jit(solution)/shard_map/convert_element_type | solution.py:124
  88.2 0.0 copy-start.8
  88.2 1.0 copy-done.8
  89.2 0.8 slice.65
  90.0 1.6 %collective-permute-start.4 = (bf16[2,512,256]{2,1,0:T(8,128)(2,1)}, bf16[2,512,256]{2,1,0:T(8,128)(2,1)}, u32[]{:S(2)}, u32[]{:S(2)}) collective-permute-start(bf16[2,512,256]{2,1,0:T(8,128)(2,1)} %slice.64), channel_id=1, source_target_pairs={{0,2},{1,3},{2,0},{3,1},{4,6},{5,7},{6,4},{7,5},{8,10},{9,11},{10,... | collective-permute-start | bytes 1572872 | tf_op jit(solution)/shard_map/ppermute | solution.py:119
  91.6 0.5 collective-permute-start.6
  92.1 0.0 all-to-all-done.1
  92.1 1.3 copy.24
  93.4 1.6 %copy-done.6 = bf16[8,512,256]{2,1,0:T(8,128)(2,1)S(1)} copy-done((bf16[8,512,256]{2,1,0:T(8,128)(2,1)S(1)}, bf16[8,512,256]{2,1,0:T(8,128)(2,1)}, u32[]{:S(2)}) %copy-start.6) | copy-done | bytes 2097176
  95.0 6.1 %attention_backward.1 = (bf16[128,4096]{1,0:T(8,128)(2,1)}, bf16[256,1024]{1,0:T(8,128)(2,1)S(1)}, bf16[256,1024]{1,0:T(8,128)(2,1)S(1)}) custom-call(bf16[128,4096]{1,0:T(8,128)(2,1)S(1)} %bitcast.39, bf16[256,2048]{1,0:T(8,128)(2,1)S(1)} %maximum_maximum_fusion.k_ref.v_ref, bf16[256,2048]{1,0:T(8,128)(2,1)S(1)} %maximum_maximum_fusion.k_ref.v_ref, ...), custom_call_target="tpu_custom_call" | custom-call | tf_op jit(solution)/shard_map/attention_backward/pallas_call | solution.py:212
  101.2 0.0 copy-start.9
  101.3 1.4 %collective-permute-start.3 = (bf16[128,2048]{1,0:T(8,128)(2,1)S(1)}, bf16[128,2048]{1,0:T(8,128)(2,1)S(1)}, u32[]{:S(2)}, u32[]{:S(2)}) collective-permute-start(bf16[128,2048]{1,0:T(8,128)(2,1)S(1)} %slice.67), channel_id=1, source_target_pairs={{8,0},{16,8},{24,16},{9,1},{17,9},{25,17},{10,2},{18,10},{26,18},{... | collective-permute-start | bytes 1572872 | tf_op jit(solution)/shard_map/ppermute | solution.py:228
  102.7 0.0 collective-permute-done.4
  102.7 1.2 add_convert_fusion.3
  103.9 2.7 %collective-permute-start.5 = (bf16[1,512,256]{2,1,0:T(8,128)(2,1)S(1)}, bf16[1,512,256]{2,1,0:T(8,128)(2,1)S(1)}, u32[]{:S(2)}, u32[]{:S(2)}) collective-permute-start(bf16[1,512,256]{2,1,0:T(8,128)(2,1)S(1)} %slice.72), channel_id=1, source_target_pairs={{0,4},{1,5},{2,6},{3,7},{4,0},{5,1},{6,2},{7,3},{8,12},{9,13},{10,... | collective-permute-start | bytes 786440 | tf_op jit(solution)/shard_map/ppermute | solution.py:119
  106.6 0.0 collective-permute-done.6
  106.6 1.2 add_convert_fusion.2
  107.8 0.4 collective-permute-start.7
  108.2 0.0 collective-permute-done.3
  108.2 0.1 add_convert_fusion.4
  108.3 0.8 slice_bitcast_fusion
  109.1 16.0 %collective-permute-done.5 = bf16[1,512,256]{2,1,0:T(8,128)(2,1)S(1)} collective-permute-done((bf16[1,512,256]{2,1,0:T(8,128)(2,1)S(1)}, bf16[1,512,256]{2,1,0:T(8,128)(2,1)S(1)}, u32[]{:S(2)}, u32[]{:S(2)}) %collective-permute-start.5) | collective-permute-done | bytes 262176 | tf_op jit(solution)/shard_map/ppermute | solution.py:119
  125.2 0.1 add_bitcast_fusion.1
  125.2 5.6 %collective-permute-done.7 = bf16[1,512,256]{2,1,0:T(8,128)(2,1)S(1)} collective-permute-done((bf16[1,512,256]{2,1,0:T(8,128)(2,1)S(1)}, bf16[1,512,256]{2,1,0:T(8,128)(2,1)S(1)}, u32[]{:S(2)}, u32[]{:S(2)}) %collective-permute-start.7) | collective-permute-done | bytes 262176 | tf_op jit(solution)/shard_map/ppermute | solution.py:119
  130.8 0.1 add_bitcast_fusion
  130.9 1.0 pad_maximum_fusion
  (24 shorter events, 0.2 us)
Async XLA Ops:
  7.2 7.3 %copy-start.1 = (bf16[1,128,4096]{2,1,0:T(8,128)(2,1)S(1)}, bf16[1,128,4096]{2,1,0:T(8,128)(2,1)}, u32[]{:S(2)}) copy-start(bf16[1,128,4096]{2,1,0:T(8,128)(2,1)} %param.9) | copy-start | bytes 3145732
  7.2 27.7 %all-gather.3.cloned.1.call-start = ((), (), s32[]{:S(2)}) async-start(), calls=%async_computation.4 | async-start | bytes 2621440 | tf_op jit(solution)/shard_map/all_gather | solution.py:158
  9.0 4.3 %collective-permute-start = (bf16[128,2048]{1,0:T(8,128)(2,1)S(1)}, bf16[128,2048]{1,0:T(8,128)(2,1)S(1)}, u32[]{:S(2)}, u32[]{:S(2)}) collective-permute-start(bf16[128,2048]{1,0:T(8,128)(2,1)S(1)} %pad_maximum_fusion.1), channel_id=1, source_target_pairs={{0,8},{8,16},{16,24},{1,9},{9,17},{17,25},{2,10},{10,18},{18,26},{... | collective-permute-start | bytes 1572872 | tf_op jit(solution)/shard_map/ppermute | solution.py:155
  20.2 1.3 copy-start.5
  21.5 1.3 copy-start.3
  22.9 24.9 %all-to-all-start = ((bf16[128,4,1024]{2,0,1:T(8,128)(2,1)}), bf16[128,4,1024]{2,0,1:T(8,128)(2,1)}, u32[]{:S(2)}, u32[]{:S(2)}) async-start(bf16[128,4,1024]{2,0,1:T(8,128)(2,1)} %bitcast.33), calls=%async_computation | async-start | bytes 2097152 | tf_op jit(solution)/shard_map/all_to_all | solution.py:180
  33.2 98.7 %reduce-scatter.2.cloned.1.call-start = ((), (), s32[]{:S(2)}) async-start(), calls=%async_computation.3 | async-start | bytes 2621440 | tf_op jit(solution)/shard_map/reduce_scatter | solution.py:197
  34.9 12.9 %copy-start = (bf16[1,512,2048]{2,1,0:T(8,128)(2,1)S(1)}, bf16[1,512,2048]{2,1,0:T(8,128)(2,1)}, u32[]{:S(2)}) copy-start(bf16[1,512,2048]{2,1,0:T(8,128)(2,1)} %all-gather.3.cloned.1.call-done) | copy-start | bytes 6291460
  47.8 4.5 %copy-start.12 = (bf16[1024,2048]{1,0:T(8,128)(2,1)S(1)}, bf16[1024,2048]{1,0:T(8,128)(2,1)}, u32[]{:S(2)}) copy-start(bf16[1024,2048]{1,0:T(8,128)(2,1)} %param.12) | copy-start | bytes 12582916
  51.2 1.1 copy-start.7
  57.2 24.0 %collective-permute-start.1 = (bf16[4,512,256]{2,1,0:T(8,128)(2,1)}, bf16[4,512,256]{2,1,0:T(8,128)(2,1)}, u32[]{:S(2)}, u32[]{:S(2)}) collective-permute-start(bf16[4,512,256]{2,1,0:T(8,128)(2,1)} %copy-done.7), channel_id=1, source_target_pairs={{0,1},{1,0},{2,3},{3,2},{4,5},{5,4},{6,7},{7,6},{8,9},{9,8},{10,11... | collective-permute-start | bytes 3145736 | tf_op jit(solution)/shard_map/ppermute | solution.py:119
  63.1 23.7 %collective-permute-start.2 = (bf16[4,512,256]{2,1,0:T(8,128)(2,1)}, bf16[4,512,256]{2,1,0:T(8,128)(2,1)}, u32[]{:S(2)}, u32[]{:S(2)}) collective-permute-start(bf16[4,512,256]{2,1,0:T(8,128)(2,1)} %weight_blocks.7), channel_id=1, source_target_pairs={{0,2},{1,3},{2,0},{3,1},{4,6},{5,7},{6,4},{7,5},{8,10},{9,11},{10,... | collective-permute-start | bytes 3145736 | tf_op jit(solution)/shard_map/ppermute | solution.py:119
  64.6 27.4 %all-to-all-start.1 = ((bf16[4,128,1024]{2,1,0:T(8,128)(2,1)}), bf16[4,128,1024]{2,1,0:T(8,128)(2,1)}, u32[]{:S(2)}, u32[]{:S(2)}) async-start(bf16[4,128,1024]{2,1,0:T(8,128)(2,1)} %bitcast.42), calls=%async_computation.2 | async-start | bytes 2097152 | tf_op jit(solution)/shard_map/all_to_all | solution.py:208
  82.7 1.2 copy-start.10
  88.2 1.0 copy-start.8
  89.2 4.2 %copy-start.2 = (bf16[1,128,4096]{2,1,0:T(8,128)(2,1)S(1)}, bf16[1,128,4096]{2,1,0:T(8,128)(2,1)}, u32[]{:S(2)}) copy-start(bf16[1,128,4096]{2,1,0:T(8,128)(2,1)} %param.9) | copy-start | bytes 3145732
  89.2 4.3 %copy-start.4 = (bf16[128,4096]{1,0:T(8,128)(2,1)S(1)}, bf16[128,4096]{1,0:T(8,128)(2,1)}, u32[]{:S(2)}) copy-start(bf16[128,4096]{1,0:T(8,128)(2,1)} %copy-done.3) | copy-start | bytes 3145732
  90.0 12.7 %collective-permute-start.4 = (bf16[2,512,256]{2,1,0:T(8,128)(2,1)}, bf16[2,512,256]{2,1,0:T(8,128)(2,1)}, u32[]{:S(2)}, u32[]{:S(2)}) collective-permute-start(bf16[2,512,256]{2,1,0:T(8,128)(2,1)} %slice.64), channel_id=1, source_target_pairs={{0,2},{1,3},{2,0},{3,1},{4,6},{5,7},{6,4},{7,5},{8,10},{9,11},{10,... | collective-permute-start | bytes 1572872 | tf_op jit(solution)/shard_map/ppermute | solution.py:119
  91.6 15.0 %collective-permute-start.6 = (bf16[2,512,256]{2,1,0:T(8,128)(2,1)}, bf16[2,512,256]{2,1,0:T(8,128)(2,1)}, u32[]{:S(2)}, u32[]{:S(2)}) collective-permute-start(bf16[2,512,256]{2,1,0:T(8,128)(2,1)} %slice.65), channel_id=1, source_target_pairs={{0,1},{1,0},{2,3},{3,2},{4,5},{5,4},{6,7},{7,6},{8,9},{9,8},{10,11... | collective-permute-start | bytes 1572872 | tf_op jit(solution)/shard_map/ppermute | solution.py:119
  93.4 1.6 %copy-start.6 = (bf16[8,512,256]{2,1,0:T(8,128)(2,1)S(1)}, bf16[8,512,256]{2,1,0:T(8,128)(2,1)}, u32[]{:S(2)}) copy-start(bf16[8,512,256]{2,1,0:T(8,128)(2,1)} %copy-done.5) | copy-start | bytes 6291460
  101.1 1.6 %copy-start.11 = (bf16[4,512,256]{2,1,0:T(8,128)(2,1)S(1)}, bf16[4,512,256]{2,1,0:T(8,128)(2,1)}, u32[]{:S(2)}) copy-start(bf16[4,512,256]{2,1,0:T(8,128)(2,1)} %copy-done.10) | copy-start | bytes 3145732
  101.2 5.4 %copy-start.9 = (bf16[4,512,256]{2,1,0:T(8,128)(2,1)S(1)}, bf16[4,512,256]{2,1,0:T(8,128)(2,1)}, u32[]{:S(2)}) copy-start(bf16[4,512,256]{2,1,0:T(8,128)(2,1)} %copy-done.8) | copy-start | bytes 3145732
  101.3 6.9 %collective-permute-start.3 = (bf16[128,2048]{1,0:T(8,128)(2,1)S(1)}, bf16[128,2048]{1,0:T(8,128)(2,1)S(1)}, u32[]{:S(2)}, u32[]{:S(2)}) collective-permute-start(bf16[128,2048]{1,0:T(8,128)(2,1)S(1)} %slice.67), channel_id=1, source_target_pairs={{8,0},{16,8},{24,16},{9,1},{17,9},{25,17},{10,2},{18,10},{26,18},{... | collective-permute-start | bytes 1572872 | tf_op jit(solution)/shard_map/ppermute | solution.py:228
  103.9 21.3 %collective-permute-start.5 = (bf16[1,512,256]{2,1,0:T(8,128)(2,1)S(1)}, bf16[1,512,256]{2,1,0:T(8,128)(2,1)S(1)}, u32[]{:S(2)}, u32[]{:S(2)}) collective-permute-start(bf16[1,512,256]{2,1,0:T(8,128)(2,1)S(1)} %slice.72), channel_id=1, source_target_pairs={{0,4},{1,5},{2,6},{3,7},{4,0},{5,1},{6,2},{7,3},{8,12},{9,13},{10,... | collective-permute-start | bytes 786440 | tf_op jit(solution)/shard_map/ppermute | solution.py:119
  107.8 23.0 %collective-permute-start.7 = (bf16[1,512,256]{2,1,0:T(8,128)(2,1)S(1)}, bf16[1,512,256]{2,1,0:T(8,128)(2,1)S(1)}, u32[]{:S(2)}, u32[]{:S(2)}) collective-permute-start(bf16[1,512,256]{2,1,0:T(8,128)(2,1)S(1)} %slice.75), channel_id=1, source_target_pairs={{0,4},{1,5},{2,6},{3,7},{4,0},{5,1},{6,2},{7,3},{8,12},{9,13},{10,... | collective-permute-start | bytes 786440 | tf_op jit(solution)/shard_map/ppermute | solution.py:119
Sparse Core Ops, SparseCore 0:
  9.6 25.2 all-gather.2
  57.4 38.2 reduce-scatter.1
